TPU v7x, 256 devices: a whole 4x4x8 slice. The times are simulated.
256 devices in a mesh: row: 32 (over y, z), col: 8 (over x, core).
Axes of the slice: x: 4, y: 4, z: 8, core: 2. Of those that a mesh axis runs over, the one named last changes fastest.
Arguments:
- momentum: float32 [28672, 8192], P('row', 'col'), may hold values from -6 to 6
- gradient: bfloat16 [28672, 8192], P('row', 'col'), may hold values from -40 to 40
- old_basis: float32 [8192, 256], P('col'), may hold values from -0.0625 to 0.0625
Outputs:
- new_momentum: float32 [28672, 8192], P('row', 'col')
- new_basis: float32 [8192, 256], P('col')
- update: bfloat16 [28672, 8192], P('row', 'col')
All inputs are finite; a program needn't handle non-finite values.
Results may differ from a plain program's by a relative error of at most 0.002.
Values sent between devices are 32-bit elements; how exact they have to be, the bound alone decides.
No kernel may reach another device: no remote copies, remote signals or barrier semaphores. Data moves between devices by JAX's collectives and lax.ppermute only.
A program may use at most 128 MiB of HBM per device.

v0:
```python
import functools

import jax
import jax.numpy as jnp
from jax import lax
from jax.experimental import pallas as pl
from jax.experimental.pallas import tpu as pltpu
from jax.sharding import PartitionSpec as P

HIGHEST = lax.Precision.HIGHEST
F32 = jnp.float32
BF16 = jnp.bfloat16
HALF = 128
GROUP = 8
PANEL = 8
ROWS = 896
COLS = 1024
RANK = 256
PIECE = 112
SLAB = 256
COEFF = 32
PAIR = 80
LIMIT = pltpu.CompilerParams(vmem_limit_bytes=32 * 1024 * 1024)


def send(value, axis, move, size):
    return lax.ppermute(value, axis, [(i, move(i)) for i in range(size)])


def send_core(value):
    return send(value, "col", lambda i: i ^ 1, 8)


def send_x(value, s):
    return send(value, "col", lambda i: ((i // 2 + s) % 4) * 2 + i % 2, 8)


def send_y(value, s):
    return send(value, "row", lambda i: ((i // 8 + s) % 4) * 8 + i % 8, 32)


def send_z(value, s):
    return send(value, "row", lambda i: (i // 8) * 8 + (i % 8 + s) % 8, 32)


Z_SHIFTS = (0, 1, 2, 7)


def ring_sum(own, came):
    return (own + came[2]) + (came[1] + came[3])


def mm(a, b, ca, cb, precision=None):
    return lax.dot_general(
        a, b, (((ca,), (cb,)), ((), ())), precision=precision, preferred_element_type=F32
    )


def split(value):
    high = value.astype(BF16)
    return high, (value - high.astype(F32)).astype(BF16)


def mm3(a, b, ca, cb):
    return mm(a[0], b[0], ca, cb) + (mm(a[0], b[1], ca, cb) + mm(a[1], b[0], ca, cb))


def whole():
    return pl.BlockSpec(memory_space=pltpu.VMEM)


def in_hbm():
    return pl.BlockSpec(memory_space=pltpu.HBM)


def scalars():
    return pl.BlockSpec(memory_space=pltpu.SMEM)


def row_start(half, x, s):
    return pl.multiple_of(half * (4 * PIECE) + lax.rem(x + s, 4) * PIECE, PIECE)


def power_away_kernel(
    pos_ref, m_ref, g_ref, b_ref, out_ref, high_ref, low_ref, m_own, g_own, b_high, b_low, m_buf, g_buf, b_buf, sems, b_sem
):
    x, core = pos_ref[2], pos_ref[3]
    load = pltpu.make_async_copy(b_ref, b_buf, b_sem)
    away, own = [], []
    for s in range(4):
        there = pl.ds(s * PIECE, PIECE)
        here = pl.ds(row_start(1 - core, x, s), PIECE)
        away.append(pltpu.make_async_copy(m_ref.at[here], m_buf.at[there], sems.at[s, 0]))
        away.append(pltpu.make_async_copy(g_ref.at[here], g_buf.at[there], sems.at[s, 1]))
        here = pl.ds(row_start(core, x, s), PIECE)
        own.append(pltpu.make_async_copy(m_ref.at[here], m_own.at[there], sems.at[4 + s, 0]))
        own.append(pltpu.make_async_copy(g_ref.at[here], g_own.at[there], sems.at[4 + s, 1]))
    load.start()
    for copy in away[:4]:
        copy.start()
    load.wait()
    for copy in away[4:]:
        copy.start()
    basis = split(b_buf[...])
    b_high[...], b_low[...] = basis
    for t in range(2):
        for copy in away[4 * t : 4 * t + 4]:
            copy.wait()
        if t == 0:
            for copy in own:
                copy.start()
        rows = pl.ds(t * 2 * PIECE, 2 * PIECE)
        high, low = split(m_buf[rows] + g_buf[rows].astype(F32))
        high_ref[rows] = high
        low_ref[rows] = low
        out_ref[rows] = mm3((high, low), basis, 1, 0)
    for copy in own:
        copy.wait()


def power_away(pos, momentum, gradient, basis):
    half = (4 * PIECE, COLS)
    return pl.pallas_call(
        power_away_kernel,
        out_shape=(
            jax.ShapeDtypeStruct((4 * PIECE, RANK), F32),
            jax.ShapeDtypeStruct(half, BF16),
            jax.ShapeDtypeStruct(half, BF16),
            jax.ShapeDtypeStruct(half, F32),
            jax.ShapeDtypeStruct(half, BF16),
            jax.ShapeDtypeStruct((COLS, RANK), BF16),
            jax.ShapeDtypeStruct((COLS, RANK), BF16),
        ),
        in_specs=[scalars(), in_hbm(), in_hbm(), in_hbm()],
        out_specs=(whole(),) * 7,
        scratch_shapes=[
            pltpu.VMEM(half, F32),
            pltpu.VMEM(half, BF16),
            pltpu.VMEM((COLS, RANK), F32),
            pltpu.SemaphoreType.DMA((8, 2)),
            pltpu.SemaphoreType.DMA,
        ],
        compiler_params=LIMIT,
        name="power_away",
    )(pos, momentum, gradient, basis)


def power_own_kernel(m_ref, g_ref, b_high, b_low, out_ref, high_ref, low_ref):
    for t in range(2):
        rows = pl.ds(t * 2 * PIECE, 2 * PIECE)
        high, low = split(m_ref[rows] + g_ref[rows].astype(F32))
        high_ref[rows] = high
        low_ref[rows] = low
        out_ref[rows] = mm3((high, low), (b_high[...], b_low[...]), 1, 0)


def power_own(momentum, gradient, b_high, b_low):
    return pl.pallas_call(
        power_own_kernel,
        out_shape=(
            jax.ShapeDtypeStruct((4 * PIECE, RANK), F32),
            jax.ShapeDtypeStruct((4 * PIECE, COLS), BF16),
            jax.ShapeDtypeStruct((4 * PIECE, COLS), BF16),
        ),
        in_specs=[whole()] * 4,
        out_specs=(whole(),) * 3,
        compiler_params=LIMIT,
        cost_estimate=pl.CostEstimate(flops=6 * 448 * 1024 * 256, bytes_accessed=4 << 20, transcendentals=0),
        name="power_own",
    )(momentum, gradient, b_high, b_low)


def project_own_kernel(s_high, s_low, own_ref, high_ref, low_ref, total_ref, gram_ref):
    value = split(own_ref[...])
    high_ref[...], low_ref[...] = value
    gram_ref[...] = mm3(value, value, 0, 0)
    for t in range(4):
        columns = pl.ds(t * SLAB, SLAB)
        total_ref[columns, :] = mm3((s_high[:, columns], s_low[:, columns]), value, 0, 0)


def project_own(s_high, s_low, own):
    return pl.pallas_call(
        project_own_kernel,
        out_shape=(
            jax.ShapeDtypeStruct((4 * PIECE, RANK), BF16),
            jax.ShapeDtypeStruct((4 * PIECE, RANK), BF16),
            jax.ShapeDtypeStruct((COLS, RANK), F32),
            jax.ShapeDtypeStruct((RANK, RANK), F32),
        ),
        in_specs=[whole()] * 3,
        out_specs=(whole(),) * 4,
        compiler_params=LIMIT,
        cost_estimate=pl.CostEstimate(flops=6 * 448 * 1280 * 256, bytes_accessed=4 << 20, transcendentals=0),
        name="project_own",
    )(s_high, s_low, own)


def fill(z, target, total_ref, gram_ref, out0_ref, out1_ref):
    for out_ref, position, a in ((out0_ref, 0, 1), (out0_ref, 1, 2), (out1_ref, 0, 3), (out1_ref, 1, 0)):
        for b in range(2):
            source = lax.rem(z + Z_SHIFTS[a], 4) + 4 * b
            place = position * PAIR
            from_total = pl.ds(pl.multiple_of(source * COEFF, COEFF), COEFF)
            from_gram = pl.ds(pl.multiple_of((target * 8 + source) * GROUP, GROUP), GROUP)
            out_ref[pl.ds(place + b * COEFF, COEFF), :] = total_ref[from_total, :]
            out_ref[pl.ds(place + 2 * COEFF + b * GROUP, GROUP), :] = gram_ref[from_gram, :]


def project_target(y, shift, s_high, s_low, value, total_ref, buf):
    target = lax.rem(y + shift, 4)
    columns = pl.ds(pl.multiple_of(target * SLAB, SLAB), SLAB)
    buf[...] = total_ref[columns, :] + mm3((s_high[:, columns], s_low[:, columns]), value, 0, 0)
    return target


def project_far_kernel(
    pos_ref, s_high, s_low, other_ref, total_ref, gram_ref, high_ref, low_ref, sum_ref, out0_ref, out1_ref, buf
):
    y, z = pos_ref[0], pos_ref[1]
    value = split(other_ref[...])
    high_ref[...], low_ref[...] = value
    sum_ref[...] = gram_ref[...] + mm3(value, value, 0, 0)
    target = project_target(y, 2, s_high, s_low, value, total_ref, buf)
    fill(z, target, buf, sum_ref, out0_ref, out1_ref)


def project_far(pos, s_high, s_low, other, total, gram):
    return pl.pallas_call(
        project_far_kernel,
        out_shape=(
            jax.ShapeDtypeStruct((4 * PIECE, RANK), BF16),
            jax.ShapeDtypeStruct((4 * PIECE, RANK), BF16),
            jax.ShapeDtypeStruct((RANK, RANK), F32),
            jax.ShapeDtypeStruct((2 * PAIR, RANK), F32),
            jax.ShapeDtypeStruct((2 * PAIR, RANK), F32),
        ),
        in_specs=[scalars()] + [whole()] * 5,
        out_specs=(whole(),) * 5,
        scratch_shapes=[pltpu.VMEM((SLAB, RANK), F32)],
        compiler_params=LIMIT,
        name="project_far",
    )(pos, s_high, s_low, other, total, gram)


def project_kernel(pos_ref, s_high, s_low, high_ref, low_ref, total_ref, gram_ref, *refs):
    y, z = pos_ref[0], pos_ref[1]
    value = (high_ref[...], low_ref[...])
    for k, shift in enumerate((0, 1, 3)):
        buf = refs[6 + k]
        target = project_target(y, shift, s_high, s_low, value, total_ref, buf)
        fill(z, target, buf, gram_ref, refs[2 * k], refs[2 * k + 1])


def project(pos, s_high, s_low, high, low, total, gram):
    return pl.pallas_call(
        project_kernel,
        out_shape=(jax.ShapeDtypeStruct((2 * PAIR, RANK), F32),) * 6,
        in_specs=[scalars()] + [whole()] * 6,
        out_specs=(whole(),) * 6,
        scratch_shapes=[pltpu.VMEM((SLAB, RANK), F32)] * 3,
        compiler_params=LIMIT,
        cost_estimate=pl.CostEstimate(flops=6 * 448 * 768 * 256, bytes_accessed=4 << 20, transcendentals=0),
        name="project",
    )(pos, s_high, s_low, high, low, total, gram)


def splat_row(value, row):
    return jnp.broadcast_to(value[row : row + 1, :], value.shape)


def splat_col(value, col):
    return jnp.broadcast_to(value[:, col : col + 1], value.shape)


def owner(y, z, j, a, b):
    from_z = lax.rem(z + 8 - Z_SHIFTS[a], 4) + 4 * b
    return lax.rem(y + 4 - j, 4) * 8 + from_z


def inverse_factor(groups):
    lane = lax.broadcasted_iota(jnp.int32, (GROUP, HALF), 1)
    sub = lax.broadcasted_iota(jnp.int32, (GROUP, HALF), 0)
    groups = list(groups)
    count = len(groups)
    result = []
    kept_rows, factor_rows = [], []
    for g in range(count):
        base = g * GROUP
        inside = (lane >= base) & (lane < base + GROUP)
        pivot = groups[g]
        cols = [splat_col(pivot, base + a) for a in range(GROUP)]
        s = [[splat_row(cols[a], b) if b >= a else None for a in range(GROUP)] for b in range(GROUP)]
        low = [[None] * GROUP for _ in range(GROUP)]
        inverse = []
        for a in range(GROUP):
            inverse.append(1.0 / s[a][a])
            for b in range(a + 1, GROUP):
                low[b][a] = s[b][a] * inverse[a]
            for b in range(a + 1, GROUP):
                for c in range(a + 1, b + 1):
                    s[b][c] = s[b][c] - low[b][a] * s[c][a]
        outside = jnp.where(inside, 0.0, pivot)
        rows = []
        for a in range(GROUP):
            row = splat_row(outside, a)
            for e in range(a):
                row = row - low[a][e] * rows[e]
            rows.append(jnp.where(lane == base + a, 1.0, row))
        last = (g // PANEL + 1) * PANEL
        for i in range(g + 1, last):
            here = groups[i]
            kept = jnp.where(inside, 0.0, here)
            factors = []
            for a in range(GROUP):
                c = splat_col(here, base + a)
                for e in range(a):
                    c = c - factors[e] * s[a][e]
                factors.append(c * inverse[a])
            for a in range(GROUP):
                kept = kept - factors[a] * rows[a]
            groups[i] = kept
        final = jnp.zeros_like(pivot)
        plain = jnp.zeros_like(pivot)
        scaled = jnp.zeros_like(pivot)
        for a in range(GROUP):
            final = jnp.where(sub == a, rows[a] * lax.rsqrt(s[a][a]), final)
            plain = jnp.where(sub == a, rows[a], plain)
            scaled = jnp.where(sub == a, rows[a] * inverse[a], scaled)
        kept_rows.append(jnp.where((lane >= base) & (lane < last * GROUP) & (lane > sub + base), 0.0, plain))
        factor_rows.append(scaled)
        if g + 1 == last and last < count:
            change = mm(jnp.concatenate(factor_rows), jnp.concatenate(kept_rows), 0, 0, HIGHEST)
            start = (last - PANEL) * GROUP
            panel = (lane >= start) & (lane < last * GROUP)
            for i in range(last, count):
                groups[i] = jnp.where(panel, 0.0, groups[i]) - change[GROUP * i : GROUP * (i + 1), :]
            kept_rows, factor_rows = [], []
        result.append(jnp.where(lane <= sub + base, final, 0.0))
    return result


def factor_kernel(pos_ref, p0, p1, p2, p3, p0_high, p0_low, p1_high, p1_low, inverse_ref, high_ref, low_ref, gram):
    y, z = pos_ref[0], pos_ref[1]
    for j, piece in enumerate((p0, p1, p2, p3)):
        for a in range(4):
            for b in range(2):
                to_gram = pl.ds(pl.multiple_of(owner(y, z, j, a, b) * GROUP, GROUP), GROUP)
                gram[to_gram, :] = piece[pl.ds((2 * a + b) * GROUP, GROUP), :]

    def rows_of(value):
        return [value[GROUP * g : GROUP * (g + 1), :] for g in range(HALF // GROUP)]

    w11 = jnp.concatenate(inverse_factor(rows_of(gram[:HALF, :HALF])), axis=0)
    l21 = mm(gram[HALF:, :HALF], w11, 1, 1, HIGHEST)
    rest = gram[HALF:, HALF:] - mm(l21, l21, 1, 1, HIGHEST)
    w22 = jnp.concatenate(inverse_factor(rows_of(rest)), axis=0)
    w21 = -mm(w22, mm(l21, w11, 1, 0, HIGHEST), 1, 0, HIGHEST)
    inverse_ref[:HALF, :HALF] = w11
    inverse_ref[:HALF, HALF:] = jnp.zeros_like(w11)
    inverse_ref[HALF:, :HALF] = w21
    inverse_ref[HALF:, HALF:] = w22
    inverse = split(inverse_ref[...])
    for t, (p_high, p_low) in enumerate(((p0_high, p0_low), (p1_high, p1_low))):
        rows = pl.ds(t * 4 * PIECE, 4 * PIECE)
        high_ref[rows], low_ref[rows] = split(mm3((p_high[...], p_low[...]), inverse, 1, 1))


def factor(pos, pieces, powered):
    return pl.pallas_call(
        factor_kernel,
        out_shape=(
            jax.ShapeDtypeStruct((RANK, RANK), F32),
            jax.ShapeDtypeStruct((ROWS, RANK), BF16),
            jax.ShapeDtypeStruct((ROWS, RANK), BF16),
        ),
        in_specs=[scalars()] + [whole()] * 8,
        out_specs=(whole(),) * 3,
        scratch_shapes=[pltpu.VMEM((RANK, RANK), F32)],
        compiler_params=LIMIT,
        cost_estimate=pl.CostEstimate(flops=10 << 30, bytes_accessed=32 << 20, transcendentals=0),
        name="factor",
    )(pos, *pieces, *powered)


def coefficients_kernel(pos_ref, p0, p1, p2, p3, inverse_ref, coeff_ref, high_ref, low_ref, square_ref):
    y, z = pos_ref[0], pos_ref[1]
    inverse = split(inverse_ref[...])
    for j, piece in enumerate((p0, p1, p2, p3)):
        value = mm3(split(piece[...]), inverse, 1, 1)
        for a in range(4):
            for b in range(2):
                place = pl.ds(pl.multiple_of(owner(y, z, j, a, b) * COEFF, COEFF), COEFF)
                coeff_ref[place, :] = value[(2 * a + b) * COEFF : (2 * a + b + 1) * COEFF]
    value = coeff_ref[...]
    high_ref[...], low_ref[...] = split(value)
    square_ref[...] = jnp.sum(value * value, axis=0, keepdims=True)


def coefficients_of(pos, pieces, inverse):
    return pl.pallas_call(
        coefficients_kernel,
        out_shape=(
            jax.ShapeDtypeStruct((COLS, RANK), F32),
            jax.ShapeDtypeStruct((COLS, RANK), BF16),
            jax.ShapeDtypeStruct((COLS, RANK), BF16),
            jax.ShapeDtypeStruct((1, RANK), F32),
        ),
        in_specs=[scalars()] + [whole()] * 5,
        out_specs=(whole(),) * 4,
        compiler_params=LIMIT,
        name="coefficients",
    )(pos, *pieces, inverse)


def write_rows(pos_ref, half, value_ref, out_ref, sems):
    x, core = pos_ref[2], pos_ref[3]
    copies = []
    for s in range(4):
        there = pl.ds(row_start(core if half == 0 else 1 - core, x, s), PIECE)
        here = pl.ds((4 * half + s) * PIECE, PIECE)
        copies.append(pltpu.make_async_copy(value_ref.at[here], out_ref.at[there], sems.at[4 * half + s]))
        copies[-1].start()
    return copies


def feedback_kernel(pos_ref, s0_high, s0_low, s1_high, s1_low, q_ref, c_ref, out_ref, buf, sems):
    coefficients = c_ref[...]
    copies = []
    for t, (s_high, s_low) in enumerate(((s0_high, s0_low), (s1_high, s1_low))):
        rows = pl.ds(t * 4 * PIECE, 4 * PIECE)
        summed = s_high[...].astype(F32) + s_low[...].astype(F32)
        buf[rows] = summed - 0.05 * mm(q_ref[rows], coefficients, 1, 1)
        copies += write_rows(pos_ref, t, buf, out_ref, sems)
    for copy in copies:
        copy.wait()


def feedback(pos, summed, high, coefficients):
    return pl.pallas_call(
        feedback_kernel,
        out_shape=jax.ShapeDtypeStruct((ROWS, COLS), F32),
        in_specs=[scalars()] + [whole()] * 6,
        out_specs=in_hbm(),
        scratch_shapes=[pltpu.VMEM((ROWS, COLS), F32), pltpu.SemaphoreType.DMA((8,))],
        compiler_params=LIMIT,
        cost_estimate=pl.CostEstimate(flops=4 * 896 * 1024 * 256, bytes_accessed=10 << 20, transcendentals=0),
        name="feedback",
    )(pos, *summed, high, coefficients)


def update_kernel(
    scale, pos_ref, high_ref, low_ref, c_ref, c_high, c_low, s_ref, basis_ref, out_ref, b_buf, buf, b_sem, sems
):
    norm = 1.0 / jnp.sqrt(s_ref[...] + 1e-6)
    b_buf[...] = c_ref[...] * norm
    store = pltpu.make_async_copy(b_buf, basis_ref, b_sem)
    store.start()
    coefficients = (c_high[...], c_low[...])
    copies = []
    for t in range(2):
        rows = pl.ds(t * 4 * PIECE, 4 * PIECE)
        q = split((high_ref[rows].astype(F32) + low_ref[rows].astype(F32)) * norm)
        buf[rows] = (scale * mm3(q, coefficients, 1, 1)).astype(BF16)
        copies += write_rows(pos_ref, t, buf, out_ref, sems)
    store.wait()
    for copy in copies:
        copy.wait()


def update(pos, high, low, coefficients, c_high, c_low, squares, scale):
    return pl.pallas_call(
        functools.partial(update_kernel, scale),
        out_shape=(
            jax.ShapeDtypeStruct((COLS, RANK), F32),
            jax.ShapeDtypeStruct((ROWS, COLS), BF16),
        ),
        in_specs=[scalars()] + [whole()] * 6,
        out_specs=(in_hbm(), in_hbm()),
        scratch_shapes=[
            pltpu.VMEM((COLS, RANK), F32),
            pltpu.VMEM((ROWS, COLS), BF16),
            pltpu.SemaphoreType.DMA,
            pltpu.SemaphoreType.DMA((8,)),
        ],
        compiler_params=LIMIT,
        name="update",
    )(pos, high, low, coefficients, c_high, c_low, squares)


def shards(momentum, gradient, old_basis):
    row = lax.axis_index("row")
    col = lax.axis_index("col")
    arguments = (momentum, gradient, old_basis)
    momentum, gradient, old_basis = (pltpu.with_memory_space_constraint(v, pltpu.HBM) for v in arguments)
    pos = jnp.stack([row // 8, row % 8, col // 2, col % 2]).astype(jnp.int32)

    away, s1_high, s1_low, m_own, g_own, b_high, b_low = power_away(pos, momentum, gradient, old_basis)
    came = send_core(away)
    here, s0_high, s0_low = power_own(m_own, g_own, b_high, b_low)
    summed = (s0_high, s0_low, s1_high, s1_low)
    parts = [here[s * PIECE : (s + 1) * PIECE] + came[s * PIECE : (s + 1) * PIECE] for s in range(4)]
    mine = ring_sum(parts[0], [None] + [send_x(parts[s], s) for s in (1, 2, 3)])
    own = jnp.concatenate([mine] + [send_x(mine, s) for s in (3, 2, 1)])
    other = send_core(own)
    p0_high, p0_low, total, gram = project_own(s0_high, s0_low, own)
    p1_high, p1_low, gram, *far = project_far(pos, s1_high, s1_low, other, total, gram)
    own0, own1, plus0, plus1, minus0, minus1 = project(pos, s1_high, s1_low, p1_high, p1_low, total, gram)
    powered = (p0_high, p0_low, p1_high, p1_low)

    far0, far1 = send_y(far[0], 1), send_y(far[1], 3)
    near1, near0 = send_y(plus1, 1), send_y(minus0, 3)
    via0, via1 = send_y(plus0 + far0, 1), send_y(minus1 + far1, 3)
    part0 = (own0 + near0) + via0
    part1 = (own1 + near1) + via1
    came = [send_z(part0[:PAIR], 1), send_z(part0[PAIR:], 2), send_z(part1[:PAIR], 7)]
    mine = ring_sum(part1[PAIR:], [None] + came)
    mine = mine + send_z(mine, 4)

    pieces = [mine] + [send_z(mine, s) for s in Z_SHIFTS[1:]]
    gram = jnp.concatenate([piece[2 * COEFF :] for piece in pieces])
    raw = jnp.concatenate([piece[: 2 * COEFF] for piece in pieces])
    grams = [gram] + [send_y(gram, s) for s in (1, 2, 3)]
    raws = [raw] + [send_y(raw, s) for s in (1, 2, 3)]
    inverse, high, low = factor(pos, grams, powered)

    coefficients, c_high, c_low, squares = coefficients_of(pos, raws, inverse)
    squares = squares + send_core(squares)
    came = [send_x(squares, s) for s in (1, 2, 3)]
    new_momentum = feedback(pos, summed, high, c_high)
    new_momentum, *came = lax.optimization_barrier((new_momentum, *came))
    squares = ring_sum(squares, [None] + came)
    rms_scale = (28672 * 8192 / 256) ** 0.5
    new_basis, new_update = update(pos, high, low, coefficients, c_high, c_low, squares, rms_scale)
    return (new_momentum, new_basis, new_update)


def solution(mesh):
    placed = (P("row", "col"), P("row", "col"), P("col", None))
    return jax.shard_map(
        shards,
        mesh=mesh,
        in_specs=placed,
        out_specs=(P("row", "col"), P("col", None), P("row", "col")),
        check_vma=False,
    )
```

profile of v0, /device:TPU:2, one launch (start us, length us, event | category | flops | bytes accessed | tf_op | source)
XLA Modules:
  0.0 112.7 jit_solution(4292716276854207633)
XLA Ops:
  0.7 0.1 pad_add_fusion.pos_ref
  0.7 4.4 %power_away.1 = (f32[448,256]{1,0:T(8,128)S(1)}, bf16[448,1024]{1,0:T(8,128)(2,1)S(1)}, bf16[448,1024]{1,0:T(8,128)(2,1)S(1)}, f32[448,1024]{1,0:T(8,128)S(1)}, ...) custom-call(s32[4]{0:T(128)S(1)} %pad_add_fusion.pos_ref, ...), custom_call_target="tpu_custom_call" | custom-call | tf_op jit(solution)/shard_map/power_away/pallas_call | solution.py:123
  5.1 0.1 collective-permute-start
  5.2 1.0 power_own.1
  6.3 0.8 collective-permute-done
  7.1 2.3 %collective-permute-start.3 = (f32[112,256]{1,0:T(8,128)S(1)}, f32[112,256]{1,0:T(8,128)S(1)}, u32[]{:S(2)}, u32[]{:S(2)}) collective-permute-start(f32[112,256]{1,0:T(8,128)S(1)} %get-tuple-element.79), channel_id=1, source_target_pairs={{0,6},{1,7},{2,0},{3,1},{4,2},{5,3},{6,4},{7,5},{8,14},{9,15},{10,... | collective-permute-start | bytes 344072 | tf_op jit(solution)/shard_map/ppermute | solution.py:27
  9.4 3.1 %collective-permute-start.1 = (f32[112,256]{1,0:T(8,128)S(1)}, f32[112,256]{1,0:T(8,128)S(1)}, u32[]{:S(2)}, u32[]{:S(2)}) collective-permute-start(f32[112,256]{1,0:T(8,128)S(1)} %get-tuple-element.81), channel_id=1, source_target_pairs={{0,4},{1,5},{2,6},{3,7},{4,0},{5,1},{6,2},{7,3},{8,12},{9,13},{10,... | collective-permute-start | bytes 344072 | tf_op jit(solution)/shard_map/ppermute | solution.py:27
  12.5 2.9 %collective-permute-done.2 = f32[112,256]{1,0:T(8,128)S(1)} collective-permute-done((f32[112,256]{1,0:T(8,128)S(1)}, f32[112,256]{1,0:T(8,128)S(1)}, u32[]{:S(2)}, u32[]{:S(2)}) %collective-permute-start.2) | collective-permute-done | bytes 114720 | tf_op jit(solution)/shard_map/ppermute | solution.py:27
  15.5 0.4 collective-permute-done.1
  15.9 2.5 %collective-permute-start.6 = (f32[112,256]{1,0:T(8,128)S(1)}, f32[112,256]{1,0:T(8,128)S(1)}, u32[]{:S(2)}, u32[]{:S(2)}) collective-permute-start(f32[112,256]{1,0:T(8,128)S(1)} %fusion.1), channel_id=1, source_target_pairs={{0,2},{1,3},{2,4},{3,5},{4,6},{5,7},{6,0},{7,1},{8,10},{9,11},{10,... | collective-permute-start | bytes 344072 | tf_op jit(solution)/shard_map/ppermute | solution.py:27
  18.4 2.8 %collective-permute-start.5 = (f32[112,256]{1,0:T(8,128)S(1)}, f32[112,256]{1,0:T(8,128)S(1)}, u32[]{:S(2)}, u32[]{:S(2)}) collective-permute-start(f32[112,256]{1,0:T(8,128)S(1)} %fusion.1), channel_id=1, source_target_pairs={{0,4},{1,5},{2,6},{3,7},{4,0},{5,1},{6,2},{7,3},{8,12},{9,13},{10,... | collective-permute-start | bytes 344072 | tf_op jit(solution)/shard_map/ppermute | solution.py:27
  21.2 0.3 collective-permute-start.4
  21.6 1.2 %collective-permute-done.6 = f32[112,256]{1,0:T(8,128)S(1)} collective-permute-done((f32[112,256]{1,0:T(8,128)S(1)}, f32[112,256]{1,0:T(8,128)S(1)}, u32[]{:S(2)}, u32[]{:S(2)}) %collective-permute-start.6) | collective-permute-done | bytes 114720 | tf_op jit(solution)/shard_map/ppermute | solution.py:27
  22.8 2.1 %collective-permute-done.5 = f32[112,256]{1,0:T(8,128)S(1)} collective-permute-done((f32[112,256]{1,0:T(8,128)S(1)}, f32[112,256]{1,0:T(8,128)S(1)}, u32[]{:S(2)}, u32[]{:S(2)}) %collective-permute-start.5) | collective-permute-done | bytes 114720 | tf_op jit(solution)/shard_map/ppermute | solution.py:27
  24.9 1.2 %collective-permute-done.4 = f32[112,256]{1,0:T(8,128)S(1)} collective-permute-done((f32[112,256]{1,0:T(8,128)S(1)}, f32[112,256]{1,0:T(8,128)S(1)}, u32[]{:S(2)}, u32[]{:S(2)}) %collective-permute-start.4) | collective-permute-done | bytes 114720 | tf_op jit(solution)/shard_map/ppermute | solution.py:27
  26.1 0.1 collective-permute-start.7
  26.2 1.3 %project_own.1 = (bf16[448,256]{1,0:T(8,128)(2,1)S(1)}, bf16[448,256]{1,0:T(8,128)(2,1)S(1)}, f32[1024,256]{1,0:T(8,128)S(1)}, f32[256,256]{1,0:T(8,128)S(1)}) custom-call(bf16[448,1024]{1,0:T(8,128)(2,1)S(1)} %get-tuple-element.45.s_high.s0_high, bf16[448,1024]{1,0:T(8,128)(2,1)S(1)} %get-tuple-element.46.s_low.s0_low, f32[448,256]{1,0:T(8,128)S(1)} %pad_maximum_fusion.own_ref), custom_call_target="tpu_custom_call" | custom-call | flops 880803840 | bytes 4194304 | tf_op jit(solution)/shard_map/project_own/pallas_call | solution.py:183
  27.5 0.5 collective-permute-done.7.other_ref
  28.0 1.2 %project_far.1 = (bf16[448,256]{1,0:T(8,128)(2,1)S(1)}, bf16[448,256]{1,0:T(8,128)(2,1)S(1)}, f32[256,256]{1,0:T(8,128)S(1)}, f32[160,256]{1,0:T(8,128)S(1)}, f32[160,256]{1,0:T(8,128)S(1)}) custom-call(s32[4]{0:T(128)S(1)} %pad_add_fusion.pos_ref, bf16[448,1024]{1,0:T(8,128)(2,1)S(1)} %get-tuple-element.47.s_high.s1_high, ...), custom_call_target="tpu_custom_call" | custom-call | tf_op jit(solution)/shard_map/project_far/pallas_call | solution.py:229
  29.3 3.3 %collective-permute-start.9 = (f32[160,256]{1,0:T(8,128)S(1)}, f32[160,256]{1,0:T(8,128)S(1)}, u32[]{:S(2)}, u32[]{:S(2)}) collective-permute-start(f32[160,256]{1,0:T(8,128)S(1)} %get-tuple-element.59), channel_id=1, source_target_pairs={{0,192},{8,200},{16,208},{24,216},{32,224},{40,232},{48,240},{56,2... | collective-permute-start | bytes 491528 | tf_op jit(solution)/shard_map/ppermute | solution.py:27
  32.6 1.5 %project.1 = (f32[160,256]{1,0:T(8,128)S(1)}, f32[160,256]{1,0:T(8,128)S(1)}, f32[160,256]{1,0:T(8,128)S(1)}, f32[160,256]{1,0:T(8,128)S(1)}, f32[160,256]{1,0:T(8,128)S(1)}, /*index=5*/f32[160,256]{1,0:T(8,128)S(1)}) custom-call(s32[4]{0:T(128)S(1)} %pad_add_fusion.pos_ref, bf16[448,1024]{1,0:T(8,128)(2,1)S(1)} %get-tuple-element.47.s_high.s1_high, ...), custom_call_target="tpu_custom_call" | custom-call | flops 528482304 | bytes 4194304 | tf_op jit(solution)/shard_map/project/pallas_call | solution.py:256
  34.0 0.8 collective-permute-start.8
  34.9 1.4 %collective-permute-done.9 = f32[160,256]{1,0:T(8,128)S(1)} collective-permute-done((f32[160,256]{1,0:T(8,128)S(1)}, f32[160,256]{1,0:T(8,128)S(1)}, u32[]{:S(2)}, u32[]{:S(2)}) %collective-permute-start.9) | collective-permute-done | bytes 163872 | tf_op jit(solution)/shard_map/ppermute | solution.py:27
  36.3 3.8 %collective-permute-start.10 = (f32[160,256]{1,0:T(8,128)S(1)}, f32[160,256]{1,0:T(8,128)S(1)}, u32[]{:S(2)}, u32[]{:S(2)}) collective-permute-start(f32[160,256]{1,0:T(8,128)S(1)} %add.82), channel_id=1, source_target_pairs={{0,192},{8,200},{16,208},{24,216},{32,224},{40,232},{48,240},{56,2... | collective-permute-start | bytes 491528 | tf_op jit(solution)/shard_map/ppermute | solution.py:27
  40.1 0.1 collective-permute-start.11
  40.2 0.7 collective-permute-done.12
  40.9 1.4 %collective-permute-start.13 = (f32[160,256]{1,0:T(8,128)S(1)}, f32[160,256]{1,0:T(8,128)S(1)}, u32[]{:S(2)}, u32[]{:S(2)}) collective-permute-start(f32[160,256]{1,0:T(8,128)S(1)} %add.85), channel_id=1, source_target_pairs={{0,64},{8,72},{16,80},{24,88},{32,96},{40,104},{48,112},{56,120},{... | collective-permute-start | bytes 491528 | tf_op jit(solution)/shard_map/ppermute | solution.py:27
  42.2 1.0 collective-permute-done.8
  43.3 1.5 %collective-permute-done.10 = f32[160,256]{1,0:T(8,128)S(1)} collective-permute-done((f32[160,256]{1,0:T(8,128)S(1)}, f32[160,256]{1,0:T(8,128)S(1)}, u32[]{:S(2)}, u32[]{:S(2)}) %collective-permute-start.10) | collective-permute-done | bytes 163872 | tf_op jit(solution)/shard_map/ppermute | solution.py:27
  44.8 5.9 %collective-permute-start.16 = (f32[80,256]{1,0:T(8,128)S(1)}, f32[80,256]{1,0:T(8,128)S(1)}, u32[]{:S(2)}, u32[]{:S(2)}) collective-permute-start(f32[80,256]{1,0:T(8,128)S(1)} %slice.87), channel_id=1, source_target_pairs={{0,56},{8,0},{16,8},{24,16},{32,24},{40,32},{48,40},{56,48},{64,12... | collective-permute-start | bytes 245768 | tf_op jit(solution)/shard_map/ppermute | solution.py:27
  50.7 0.0 collective-permute-done.11
  50.7 0.0 collective-permute-done.13
  50.8 0.1 collective-permute-start.15
  50.9 1.9 %collective-permute-start.14 = (f32[80,256]{1,0:T(8,128)S(1)}, f32[80,256]{1,0:T(8,128)S(1)}, u32[]{:S(2)}, u32[]{:S(2)}) collective-permute-start(f32[80,256]{1,0:T(8,128)S(1)} %get-tuple-element.83), channel_id=1, source_target_pairs={{0,16},{8,24},{16,32},{24,40},{32,48},{40,56},{48,0},{56,8},{64,80... | collective-permute-start | bytes 245768 | tf_op jit(solution)/shard_map/ppermute | solution.py:27
  52.8 3.7 %collective-permute-done.15 = f32[80,256]{1,0:T(8,128)S(1)} collective-permute-done((f32[80,256]{1,0:T(8,128)S(1)}, f32[80,256]{1,0:T(8,128)S(1)}, u32[]{:S(2)}, u32[]{:S(2)}) %collective-permute-start.15) | collective-permute-done | bytes 81952 | tf_op jit(solution)/shard_map/ppermute | solution.py:27
  56.5 2.6 %collective-permute-done.14 = f32[80,256]{1,0:T(8,128)S(1)} collective-permute-done((f32[80,256]{1,0:T(8,128)S(1)}, f32[80,256]{1,0:T(8,128)S(1)}, u32[]{:S(2)}, u32[]{:S(2)}) %collective-permute-start.14) | collective-permute-done | bytes 81952 | tf_op jit(solution)/shard_map/ppermute | solution.py:27
  59.1 4.4 %collective-permute-start.17 = (f32[80,256]{1,0:T(8,128)S(1)}, f32[80,256]{1,0:T(8,128)S(1)}, u32[]{:S(2)}, u32[]{:S(2)}) collective-permute-start(f32[80,256]{1,0:T(8,128)S(1)} %fusion.2), channel_id=1, source_target_pairs={{0,32},{8,40},{16,48},{24,56},{32,0},{40,8},{48,16},{56,24},{64,96... | collective-permute-start | bytes 245768 | tf_op jit(solution)/shard_map/ppermute | solution.py:27
  63.5 4.9 %collective-permute-done.17 = f32[80,256]{1,0:T(8,128)S(1)} collective-permute-done((f32[80,256]{1,0:T(8,128)S(1)}, f32[80,256]{1,0:T(8,128)S(1)}, u32[]{:S(2)}, u32[]{:S(2)}) %collective-permute-start.17) | collective-permute-done | bytes 81952 | tf_op jit(solution)/shard_map/ppermute | solution.py:27
  68.5 0.1 collective-permute-start.20
  68.5 0.5 collective-permute-start.19
  69.1 1.5 %collective-permute-start.18 = (f32[80,256]{1,0:T(8,128)S(1)}, f32[80,256]{1,0:T(8,128)S(1)}, u32[]{:S(2)}, u32[]{:S(2)}) collective-permute-start(f32[80,256]{1,0:T(8,128)S(1)} %add.90), channel_id=1, source_target_pairs={{0,8},{8,16},{16,24},{24,32},{32,40},{40,48},{48,56},{56,0},{64,72... | collective-permute-start | bytes 245768 | tf_op jit(solution)/shard_map/ppermute | solution.py:27
  70.6 2.4 %collective-permute-done.20 = f32[80,256]{1,0:T(8,128)S(1)} collective-permute-done((f32[80,256]{1,0:T(8,128)S(1)}, f32[80,256]{1,0:T(8,128)S(1)}, u32[]{:S(2)}, u32[]{:S(2)}) %collective-permute-start.20) | collective-permute-done | bytes 81952 | tf_op jit(solution)/shard_map/ppermute | solution.py:27
  73.0 3.1 %collective-permute-done.19 = f32[80,256]{1,0:T(8,128)S(1)} collective-permute-done((f32[80,256]{1,0:T(8,128)S(1)}, f32[80,256]{1,0:T(8,128)S(1)}, u32[]{:S(2)}, u32[]{:S(2)}) %collective-permute-start.19) | collective-permute-done | bytes 81952 | tf_op jit(solution)/shard_map/ppermute | solution.py:27
  76.1 0.9 collective-permute-done.18
  77.0 4.1 %collective-permute-start.23 = (f32[64,256]{1,0:T(8,128)S(1)}, f32[64,256]{1,0:T(8,128)S(1)}, u32[]{:S(2)}, u32[]{:S(2)}) collective-permute-start(f32[64,256]{1,0:T(8,128)S(1)} %pad_maximum_fusion.2.p0), channel_id=1, source_target_pairs={{0,192},{8,200},{16,208},{24,216},{32,224},{40,232},{48,240},{56,2... | collective-permute-start | bytes 196616 | tf_op jit(solution)/shard_map/ppermute | solution.py:27
  81.0 0.0 collective-permute-start.22
  81.0 1.0 collective-permute-start.21
  82.0 2.4 %collective-permute-start.26 = (f32[256,256]{1,0:T(8,128)S(1)}, f32[256,256]{1,0:T(8,128)S(1)}, u32[]{:S(2)}, u32[]{:S(2)}) collective-permute-start(f32[256,256]{1,0:T(8,128)S(1)} %pad_maximum_fusion.1.p0), channel_id=1, source_target_pairs={{0,192},{8,200},{16,208},{24,216},{32,224},{40,232},{48,240},{56,2... | collective-permute-start | bytes 786440 | tf_op jit(solution)/shard_map/ppermute | solution.py:27
  84.4 2.3 %collective-permute-start.25 = (f32[256,256]{1,0:T(8,128)S(1)}, f32[256,256]{1,0:T(8,128)S(1)}, u32[]{:S(2)}, u32[]{:S(2)}) collective-permute-start(f32[256,256]{1,0:T(8,128)S(1)} %pad_maximum_fusion.1.p0), channel_id=1, source_target_pairs={{0,128},{8,136},{16,144},{24,152},{32,160},{40,168},{48,176},{56,1... | collective-permute-start | bytes 786440 | tf_op jit(solution)/shard_map/ppermute | solution.py:27
  86.7 0.0 collective-permute-done.23.p3
  86.7 0.0 collective-permute-start.24
  86.7 0.8 collective-permute-done.22.p2
  87.6 0.4 collective-permute-done.21.p1
  88.0 9.8 %factor.1 = (f32[256,256]{1,0:T(8,128)S(1)}, bf16[896,256]{1,0:T(8,128)(2,1)S(1)}, bf16[896,256]{1,0:T(8,128)(2,1)S(1)}) custom-call(s32[4]{0:T(128)S(1)} %pad_add_fusion.pos_ref, f32[64,256]{1,0:T(8,128)S(1)} %pad_maximum_fusion.2.p0, f32[64,256]{1,0:T(8,128)S(1)} %collective-permute-done.21.p1, f32[64,256]{1,0:T(8,128)S(1)} %collective-permute-done.22.p2, ...), custom_call_target="tpu_custom_call" | custom-call | flops 10737418240 | bytes 33554432 | tf_op jit(solution)/shard_map/factor/pallas_call | solution.py:370
  97.8 0.0 collective-permute-done.26.p3
  97.8 0.0 collective-permute-done.24.p1
  97.8 1.6 %coefficients.1 = (f32[1024,256]{1,0:T(8,128)S(1)}, bf16[1024,256]{1,0:T(8,128)(2,1)S(1)}, bf16[1024,256]{1,0:T(8,128)(2,1)S(1)}, f32[1,256]{1,0:T(1,128)S(1)}) custom-call(s32[4]{0:T(128)S(1)} %pad_add_fusion.pos_ref, f32[256,256]{1,0:T(8,128)S(1)} %pad_maximum_fusion.1.p0, f32[256,256]{1,0:T(8,128)S(1)} %collective-permute-done.24.p1, ...), custom_call_target="tpu_custom_call" | custom-call | tf_op jit(solution)/shard_map/coefficients/pallas_call | solution.py:401
  99.4 0.1 collective-permute-start.27
  99.5 1.1 collective-permute-done.27
  100.7 1.6 %collective-permute-start.30 = (f32[1,256]{1,0:T(1,128)S(1)}, f32[1,256]{1,0:T(1,128)S(1)}, u32[]{:S(2)}, u32[]{:S(2)}) collective-permute-start(f32[1,256]{1,0:T(1,128)S(1)} %add.91), channel_id=1, source_target_pairs={{0,6},{1,7},{2,0},{3,1},{4,2},{5,3},{6,4},{7,5},{8,14},{9,15},{10,... | collective-permute-start | bytes 3080 | tf_op jit(solution)/shard_map/ppermute | solution.py:27
  102.2 1.2 %collective-permute-start.29 = (f32[1,256]{1,0:T(1,128)S(1)}, f32[1,256]{1,0:T(1,128)S(1)}, u32[]{:S(2)}, u32[]{:S(2)}) collective-permute-start(f32[1,256]{1,0:T(1,128)S(1)} %add.91), channel_id=1, source_target_pairs={{0,4},{1,5},{2,6},{3,7},{4,0},{5,1},{6,2},{7,3},{8,12},{9,13},{10,... | collective-permute-start | bytes 3080 | tf_op jit(solution)/shard_map/ppermute | solution.py:27
  103.4 2.6 %collective-permute-start.28 = (f32[1,256]{1,0:T(1,128)S(1)}, f32[1,256]{1,0:T(1,128)S(1)}, u32[]{:S(2)}, u32[]{:S(2)}) collective-permute-start(f32[1,256]{1,0:T(1,128)S(1)} %add.91), channel_id=1, source_target_pairs={{0,2},{1,3},{2,4},{3,5},{4,6},{5,7},{6,0},{7,1},{8,10},{9,11},{10,... | collective-permute-start | bytes 3080 | tf_op jit(solution)/shard_map/ppermute | solution.py:27
  106.0 2.9 %feedback.1 = f32[896,1024]{1,0:T(8,128)} custom-call(s32[4]{0:T(128)S(1)} %pad_add_fusion.pos_ref, bf16[448,1024]{1,0:T(8,128)(2,1)S(1)} %get-tuple-element.45.s_high.s0_high, bf16[448,1024]{1,0:T(8,128)(2,1)S(1)} %get-tuple-element.46.s_low.s0_low, bf16[448,1024]{1,0:T(8,128)(2,1)S(1)} %get-tuple-element.47.s_high.s1_high, ...), custom_call_target="tpu_custom_call" | custom-call | flops 939524096 | bytes 10485760 | tf_op jit(solution)/shard_map/feedback/pallas_call | solution.py:440
  109.0 3.5 %update.1 = (f32[1024,256]{1,0:T(8,128)}, bf16[896,1024]{1,0:T(8,128)(2,1)}) custom-call(s32[4]{0:T(128)S(1)} %pad_add_fusion.pos_ref, bf16[896,256]{1,0:T(8,128)(2,1)S(1)} %get-tuple-element.66.q_ref.high_ref, bf16[896,256]{1,0:T(8,128)(2,1)S(1)} %get-tuple-element.71.low_ref, f32[1024,256]{1,0:T(8,128)S(1)} %get-tuple-element.72.c_ref, ...), custom_call_target="tpu_custom_call" | custom-call | tf_op jit(solution)/shard_map/update/pallas_call | solution.py:472
  (31 shorter events, 0.4 us)
Async XLA Ops:
  5.1 1.9 %collective-permute-start = (f32[448,256]{1,0:T(8,128)S(1)}, f32[448,256]{1,0:T(8,128)S(1)}, u32[]{:S(2)}, u32[]{:S(2)}) collective-permute-start(f32[448,256]{1,0:T(8,128)S(1)} %get-tuple-element.50), channel_id=1, source_target_pairs={{0,1},{1,0},{2,3},{3,2},{4,5},{5,4},{6,7},{7,6},{8,9},{9,8},{10,11... | collective-permute-start | bytes 1376264 | tf_op jit(solution)/shard_map/ppermute | solution.py:27
  7.1 5.4 %collective-permute-start.3 = (f32[112,256]{1,0:T(8,128)S(1)}, f32[112,256]{1,0:T(8,128)S(1)}, u32[]{:S(2)}, u32[]{:S(2)}) collective-permute-start(f32[112,256]{1,0:T(8,128)S(1)} %get-tuple-element.79), channel_id=1, source_target_pairs={{0,6},{1,7},{2,0},{3,1},{4,2},{5,3},{6,4},{7,5},{8,14},{9,15},{10,... | collective-permute-start | bytes 344072 | tf_op jit(solution)/shard_map/ppermute | solution.py:27
  9.4 6.0 %collective-permute-start.2 = (f32[112,256]{1,0:T(8,128)S(1)}, f32[112,256]{1,0:T(8,128)S(1)}, u32[]{:S(2)}, u32[]{:S(2)}) collective-permute-start(f32[112,256]{1,0:T(8,128)S(1)} %get-tuple-element.80), channel_id=1, source_target_pairs={{0,2},{1,3},{2,4},{3,5},{4,6},{5,7},{6,0},{7,1},{8,10},{9,11},{10,... | collective-permute-start | bytes 344072 | tf_op jit(solution)/shard_map/ppermute | solution.py:27
  9.4 6.4 %collective-permute-start.1 = (f32[112,256]{1,0:T(8,128)S(1)}, f32[112,256]{1,0:T(8,128)S(1)}, u32[]{:S(2)}, u32[]{:S(2)}) collective-permute-start(f32[112,256]{1,0:T(8,128)S(1)} %get-tuple-element.81), channel_id=1, source_target_pairs={{0,4},{1,5},{2,6},{3,7},{4,0},{5,1},{6,2},{7,3},{8,12},{9,13},{10,... | collective-permute-start | bytes 344072 | tf_op jit(solution)/shard_map/ppermute | solution.py:27
  15.9 6.9 %collective-permute-start.6 = (f32[112,256]{1,0:T(8,128)S(1)}, f32[112,256]{1,0:T(8,128)S(1)}, u32[]{:S(2)}, u32[]{:S(2)}) collective-permute-start(f32[112,256]{1,0:T(8,128)S(1)} %fusion.1), channel_id=1, source_target_pairs={{0,2},{1,3},{2,4},{3,5},{4,6},{5,7},{6,0},{7,1},{8,10},{9,11},{10,... | collective-permute-start | bytes 344072 | tf_op jit(solution)/shard_map/ppermute | solution.py:27
  18.4 6.5 %collective-permute-start.5 = (f32[112,256]{1,0:T(8,128)S(1)}, f32[112,256]{1,0:T(8,128)S(1)}, u32[]{:S(2)}, u32[]{:S(2)}) collective-permute-start(f32[112,256]{1,0:T(8,128)S(1)} %fusion.1), channel_id=1, source_target_pairs={{0,4},{1,5},{2,6},{3,7},{4,0},{5,1},{6,2},{7,3},{8,12},{9,13},{10,... | collective-permute-start | bytes 344072 | tf_op jit(solution)/shard_map/ppermute | solution.py:27
  21.2 4.9 %collective-permute-start.4 = (f32[112,256]{1,0:T(8,128)S(1)}, f32[112,256]{1,0:T(8,128)S(1)}, u32[]{:S(2)}, u32[]{:S(2)}) collective-permute-start(f32[112,256]{1,0:T(8,128)S(1)} %fusion.1), channel_id=1, source_target_pairs={{0,6},{1,7},{2,0},{3,1},{4,2},{5,3},{6,4},{7,5},{8,14},{9,15},{10,... | collective-permute-start | bytes 344072 | tf_op jit(solution)/shard_map/ppermute | solution.py:27
  26.1 1.9 %collective-permute-start.7 = (f32[448,256]{1,0:T(8,128)S(1)}, f32[448,256]{1,0:T(8,128)S(1)}, u32[]{:S(2)}, u32[]{:S(2)}) collective-permute-start(f32[448,256]{1,0:T(8,128)S(1)} %pad_maximum_fusion.own_ref), channel_id=1, source_target_pairs={{0,1},{1,0},{2,3},{3,2},{4,5},{5,4},{6,7},{7,6},{8,9},{9,8},{10,11... | collective-permute-start | bytes 1376264 | tf_op jit(solution)/shard_map/ppermute | solution.py:27
  29.3 7.0 %collective-permute-start.9 = (f32[160,256]{1,0:T(8,128)S(1)}, f32[160,256]{1,0:T(8,128)S(1)}, u32[]{:S(2)}, u32[]{:S(2)}) collective-permute-start(f32[160,256]{1,0:T(8,128)S(1)} %get-tuple-element.59), channel_id=1, source_target_pairs={{0,192},{8,200},{16,208},{24,216},{32,224},{40,232},{48,240},{56,2... | collective-permute-start | bytes 491528 | tf_op jit(solution)/shard_map/ppermute | solution.py:27
  32.6 8.3 %collective-permute-start.12 = (f32[160,256]{1,0:T(8,128)S(1)}, f32[160,256]{1,0:T(8,128)S(1)}, u32[]{:S(2)}, u32[]{:S(2)}) collective-permute-start(f32[160,256]{1,0:T(8,128)S(1)} %get-tuple-element.63), channel_id=1, source_target_pairs={{0,64},{8,72},{16,80},{24,88},{32,96},{40,104},{48,112},{56,120},{... | collective-permute-start | bytes 491528 | tf_op jit(solution)/shard_map/ppermute | solution.py:27
  34.0 9.2 %collective-permute-start.8 = (f32[160,256]{1,0:T(8,128)S(1)}, f32[160,256]{1,0:T(8,128)S(1)}, u32[]{:S(2)}, u32[]{:S(2)}) collective-permute-start(f32[160,256]{1,0:T(8,128)S(1)} %get-tuple-element.57), channel_id=1, source_target_pairs={{0,64},{8,72},{16,80},{24,88},{32,96},{40,104},{48,112},{56,120},{... | collective-permute-start | bytes 491528 | tf_op jit(solution)/shard_map/ppermute | solution.py:27
  36.3 8.4 %collective-permute-start.10 = (f32[160,256]{1,0:T(8,128)S(1)}, f32[160,256]{1,0:T(8,128)S(1)}, u32[]{:S(2)}, u32[]{:S(2)}) collective-permute-start(f32[160,256]{1,0:T(8,128)S(1)} %add.82), channel_id=1, source_target_pairs={{0,192},{8,200},{16,208},{24,216},{32,224},{40,232},{48,240},{56,2... | collective-permute-start | bytes 491528 | tf_op jit(solution)/shard_map/ppermute | solution.py:27
  40.1 10.6 %collective-permute-start.11 = (f32[160,256]{1,0:T(8,128)S(1)}, f32[160,256]{1,0:T(8,128)S(1)}, u32[]{:S(2)}, u32[]{:S(2)}) collective-permute-start(f32[160,256]{1,0:T(8,128)S(1)} %get-tuple-element.61), channel_id=1, source_target_pairs={{0,192},{8,200},{16,208},{24,216},{32,224},{40,232},{48,240},{56,2... | collective-permute-start | bytes 491528 | tf_op jit(solution)/shard_map/ppermute | solution.py:27
  40.9 9.9 %collective-permute-start.13 = (f32[160,256]{1,0:T(8,128)S(1)}, f32[160,256]{1,0:T(8,128)S(1)}, u32[]{:S(2)}, u32[]{:S(2)}) collective-permute-start(f32[160,256]{1,0:T(8,128)S(1)} %add.85), channel_id=1, source_target_pairs={{0,64},{8,72},{16,80},{24,88},{32,96},{40,104},{48,112},{56,120},{... | collective-permute-start | bytes 491528 | tf_op jit(solution)/shard_map/ppermute | solution.py:27
  44.8 8.0 %collective-permute-start.16 = (f32[80,256]{1,0:T(8,128)S(1)}, f32[80,256]{1,0:T(8,128)S(1)}, u32[]{:S(2)}, u32[]{:S(2)}) collective-permute-start(f32[80,256]{1,0:T(8,128)S(1)} %slice.87), channel_id=1, source_target_pairs={{0,56},{8,0},{16,8},{24,16},{32,24},{40,32},{48,40},{56,48},{64,12... | collective-permute-start | bytes 245768 | tf_op jit(solution)/shard_map/ppermute | solution.py:27
  50.8 5.7 %collective-permute-start.15 = (f32[80,256]{1,0:T(8,128)S(1)}, f32[80,256]{1,0:T(8,128)S(1)}, u32[]{:S(2)}, u32[]{:S(2)}) collective-permute-start(f32[80,256]{1,0:T(8,128)S(1)} %get-tuple-element.82), channel_id=1, source_target_pairs={{0,8},{8,16},{16,24},{24,32},{32,40},{40,48},{48,56},{56,0},{64,72... | collective-permute-start | bytes 245768 | tf_op jit(solution)/shard_map/ppermute | solution.py:27
  50.9 8.2 %collective-permute-start.14 = (f32[80,256]{1,0:T(8,128)S(1)}, f32[80,256]{1,0:T(8,128)S(1)}, u32[]{:S(2)}, u32[]{:S(2)}) collective-permute-start(f32[80,256]{1,0:T(8,128)S(1)} %get-tuple-element.83), channel_id=1, source_target_pairs={{0,16},{8,24},{16,32},{24,40},{32,48},{40,56},{48,0},{56,8},{64,80... | collective-permute-start | bytes 245768 | tf_op jit(solution)/shard_map/ppermute | solution.py:27
  59.1 9.3 %collective-permute-start.17 = (f32[80,256]{1,0:T(8,128)S(1)}, f32[80,256]{1,0:T(8,128)S(1)}, u32[]{:S(2)}, u32[]{:S(2)}) collective-permute-start(f32[80,256]{1,0:T(8,128)S(1)} %fusion.2), channel_id=1, source_target_pairs={{0,32},{8,40},{16,48},{24,56},{32,0},{40,8},{48,16},{56,24},{64,96... | collective-permute-start | bytes 245768 | tf_op jit(solution)/shard_map/ppermute | solution.py:27
  68.5 4.5 %collective-permute-start.20 = (f32[80,256]{1,0:T(8,128)S(1)}, f32[80,256]{1,0:T(8,128)S(1)}, u32[]{:S(2)}, u32[]{:S(2)}) collective-permute-start(f32[80,256]{1,0:T(8,128)S(1)} %add.90), channel_id=1, source_target_pairs={{0,56},{8,0},{16,8},{24,16},{32,24},{40,32},{48,40},{56,48},{64,12... | collective-permute-start | bytes 245768 | tf_op jit(solution)/shard_map/ppermute | solution.py:27
  68.5 7.5 %collective-permute-start.19 = (f32[80,256]{1,0:T(8,128)S(1)}, f32[80,256]{1,0:T(8,128)S(1)}, u32[]{:S(2)}, u32[]{:S(2)}) collective-permute-start(f32[80,256]{1,0:T(8,128)S(1)} %add.90), channel_id=1, source_target_pairs={{0,16},{8,24},{16,32},{24,40},{32,48},{40,56},{48,0},{56,8},{64,80... | collective-permute-start | bytes 245768 | tf_op jit(solution)/shard_map/ppermute | solution.py:27
  69.1 7.9 %collective-permute-start.18 = (f32[80,256]{1,0:T(8,128)S(1)}, f32[80,256]{1,0:T(8,128)S(1)}, u32[]{:S(2)}, u32[]{:S(2)}) collective-permute-start(f32[80,256]{1,0:T(8,128)S(1)} %add.90), channel_id=1, source_target_pairs={{0,8},{8,16},{16,24},{24,32},{32,40},{40,48},{48,56},{56,0},{64,72... | collective-permute-start | bytes 245768 | tf_op jit(solution)/shard_map/ppermute | solution.py:27
  77.0 9.8 %collective-permute-start.23 = (f32[64,256]{1,0:T(8,128)S(1)}, f32[64,256]{1,0:T(8,128)S(1)}, u32[]{:S(2)}, u32[]{:S(2)}) collective-permute-start(f32[64,256]{1,0:T(8,128)S(1)} %pad_maximum_fusion.2.p0), channel_id=1, source_target_pairs={{0,192},{8,200},{16,208},{24,216},{32,224},{40,232},{48,240},{56,2... | collective-permute-start | bytes 196616 | tf_op jit(solution)/shard_map/ppermute | solution.py:27
  81.0 6.5 %collective-permute-start.22 = (f32[64,256]{1,0:T(8,128)S(1)}, f32[64,256]{1,0:T(8,128)S(1)}, u32[]{:S(2)}, u32[]{:S(2)}) collective-permute-start(f32[64,256]{1,0:T(8,128)S(1)} %pad_maximum_fusion.2.p0), channel_id=1, source_target_pairs={{0,128},{8,136},{16,144},{24,152},{32,160},{40,168},{48,176},{56,1... | collective-permute-start | bytes 196616 | tf_op jit(solution)/shard_map/ppermute | solution.py:27
  81.0 6.9 %collective-permute-start.21 = (f32[64,256]{1,0:T(8,128)S(1)}, f32[64,256]{1,0:T(8,128)S(1)}, u32[]{:S(2)}, u32[]{:S(2)}) collective-permute-start(f32[64,256]{1,0:T(8,128)S(1)} %pad_maximum_fusion.2.p0), channel_id=1, source_target_pairs={{0,64},{8,72},{16,80},{24,88},{32,96},{40,104},{48,112},{56,120},{... | collective-permute-start | bytes 196616 | tf_op jit(solution)/shard_map/ppermute | solution.py:27
  82.0 15.7 %collective-permute-start.26 = (f32[256,256]{1,0:T(8,128)S(1)}, f32[256,256]{1,0:T(8,128)S(1)}, u32[]{:S(2)}, u32[]{:S(2)}) collective-permute-start(f32[256,256]{1,0:T(8,128)S(1)} %pad_maximum_fusion.1.p0), channel_id=1, source_target_pairs={{0,192},{8,200},{16,208},{24,216},{32,224},{40,232},{48,240},{56,2... | collective-permute-start | bytes 786440 | tf_op jit(solution)/shard_map/ppermute | solution.py:27
  84.4 13.4 %collective-permute-start.25 = (f32[256,256]{1,0:T(8,128)S(1)}, f32[256,256]{1,0:T(8,128)S(1)}, u32[]{:S(2)}, u32[]{:S(2)}) collective-permute-start(f32[256,256]{1,0:T(8,128)S(1)} %pad_maximum_fusion.1.p0), channel_id=1, source_target_pairs={{0,128},{8,136},{16,144},{24,152},{32,160},{40,168},{48,176},{56,1... | collective-permute-start | bytes 786440 | tf_op jit(solution)/shard_map/ppermute | solution.py:27
  86.7 11.1 %collective-permute-start.24 = (f32[256,256]{1,0:T(8,128)S(1)}, f32[256,256]{1,0:T(8,128)S(1)}, u32[]{:S(2)}, u32[]{:S(2)}) collective-permute-start(f32[256,256]{1,0:T(8,128)S(1)} %pad_maximum_fusion.1.p0), channel_id=1, source_target_pairs={{0,64},{8,72},{16,80},{24,88},{32,96},{40,104},{48,112},{56,120},{... | collective-permute-start | bytes 786440 | tf_op jit(solution)/shard_map/ppermute | solution.py:27
  99.4 1.2 %collective-permute-start.27 = (f32[1,256]{1,0:T(1,128)S(1)}, f32[1,256]{1,0:T(1,128)S(1)}, u32[]{:S(2)}, u32[]{:S(2)}) collective-permute-start(f32[1,256]{1,0:T(1,128)S(1)} %get-tuple-element.69), channel_id=1, source_target_pairs={{0,1},{1,0},{2,3},{3,2},{4,5},{5,4},{6,7},{7,6},{8,9},{9,8},{10,11... | collective-permute-start | bytes 3080 | tf_op jit(solution)/shard_map/ppermute | solution.py:27
  100.7 8.3 %collective-permute-start.30 = (f32[1,256]{1,0:T(1,128)S(1)}, f32[1,256]{1,0:T(1,128)S(1)}, u32[]{:S(2)}, u32[]{:S(2)}) collective-permute-start(f32[1,256]{1,0:T(1,128)S(1)} %add.91), channel_id=1, source_target_pairs={{0,6},{1,7},{2,0},{3,1},{4,2},{5,3},{6,4},{7,5},{8,14},{9,15},{10,... | collective-permute-start | bytes 3080 | tf_op jit(solution)/shard_map/ppermute | solution.py:27
  102.2 6.7 %collective-permute-start.29 = (f32[1,256]{1,0:T(1,128)S(1)}, f32[1,256]{1,0:T(1,128)S(1)}, u32[]{:S(2)}, u32[]{:S(2)}) collective-permute-start(f32[1,256]{1,0:T(1,128)S(1)} %add.91), channel_id=1, source_target_pairs={{0,4},{1,5},{2,6},{3,7},{4,0},{5,1},{6,2},{7,3},{8,12},{9,13},{10,... | collective-permute-start | bytes 3080 | tf_op jit(solution)/shard_map/ppermute | solution.py:27
  103.4 5.6 %collective-permute-start.28 = (f32[1,256]{1,0:T(1,128)S(1)}, f32[1,256]{1,0:T(1,128)S(1)}, u32[]{:S(2)}, u32[]{:S(2)}) collective-permute-start(f32[1,256]{1,0:T(1,128)S(1)} %add.91), channel_id=1, source_target_pairs={{0,2},{1,3},{2,4},{3,5},{4,6},{5,7},{6,0},{7,1},{8,10},{9,11},{10,... | collective-permute-start | bytes 3080 | tf_op jit(solution)/shard_map/ppermute | solution.py:27
where the time goes:
time: 113 us
  starting transfers between devices  50.2 us (44%)
  waiting for transfers between devices  33.7 us (30%)
  Pallas kernels  27.2 us (24%)
    ppermute x31, starting transfers between devices, send(): return lax.ppermute(value, axis, [(i, move(i)) for i in range(size)])  50.2 us
    ppermute x31, waiting for transfers between devices, send(): return lax.ppermute(value, axis, [(i, move(i)) for i in range(size)])  33.7 us
    pallas_call x1, Pallas kernels, factor(): pl.pallas_call(factor_kernel, out_shape=(jax.ShapeDtypeStruct((RANK, RANK...  9.8 us
    pallas_call x1, Pallas kernels, power_away(): pl.pallas_call(power_away_kernel, out_shape=(jax.ShapeDtypeStruct((4 * PI...  4.39 us
    pallas_call x1, Pallas kernels, update(): pl.pallas_call(functools.partial(update_kernel, scale), out_shape=(jax.Sh...  3.53 us
    pallas_call x1, Pallas kernels, feedback(): pl.pallas_call(feedback_kernel, out_shape=jax.ShapeDtypeStruct((ROWS, COL...  2.92 us
  transfers between devices with their start and end apart: 31, of which 20 were waited for; matrix products, arithmetic and copies ran while one was open for 0% of the time, Pallas kernels for 15%

commit v1 on v0

--- a/solution.py
+++ b/solution.py
@@ -340,7 +340,7 @@
     return result
 
 
-def factor_kernel(pos_ref, p0, p1, p2, p3, p0_high, p0_low, p1_high, p1_low, inverse_ref, high_ref, low_ref, gram):
+def factor_kernel(pos_ref, p0, p1, p2, p3, inverse_ref, gram):
     y, z = pos_ref[0], pos_ref[1]
     for j, piece in enumerate((p0, p1, p2, p3)):
         for a in range(4):
@@ -360,27 +360,38 @@
     inverse_ref[:HALF, HALF:] = jnp.zeros_like(w11)
     inverse_ref[HALF:, :HALF] = w21
     inverse_ref[HALF:, HALF:] = w22
+
+
+def factor(pos, pieces):
+    return pl.pallas_call(
+        factor_kernel,
+        out_shape=jax.ShapeDtypeStruct((RANK, RANK), F32),
+        in_specs=[scalars()] + [whole()] * 4,
+        out_specs=whole(),
+        scratch_shapes=[pltpu.VMEM((RANK, RANK), F32)],
+        compiler_params=LIMIT,
+        cost_estimate=pl.CostEstimate(flops=10 << 30, bytes_accessed=32 << 20, transcendentals=0),
+        name="factor",
+    )(pos, *pieces)
+
+
+def orthonormal_kernel(p0_high, p0_low, p1_high, p1_low, inverse_ref, high_ref, low_ref):
     inverse = split(inverse_ref[...])
     for t, (p_high, p_low) in enumerate(((p0_high, p0_low), (p1_high, p1_low))):
         rows = pl.ds(t * 4 * PIECE, 4 * PIECE)
         high_ref[rows], low_ref[rows] = split(mm3((p_high[...], p_low[...]), inverse, 1, 1))
 
 
-def factor(pos, pieces, powered):
-    return pl.pallas_call(
-        factor_kernel,
-        out_shape=(
-            jax.ShapeDtypeStruct((RANK, RANK), F32),
-            jax.ShapeDtypeStruct((ROWS, RANK), BF16),
-            jax.ShapeDtypeStruct((ROWS, RANK), BF16),
-        ),
-        in_specs=[scalars()] + [whole()] * 8,
-        out_specs=(whole(),) * 3,
-        scratch_shapes=[pltpu.VMEM((RANK, RANK), F32)],
-        compiler_params=LIMIT,
-        cost_estimate=pl.CostEstimate(flops=10 << 30, bytes_accessed=32 << 20, transcendentals=0),
-        name="factor",
-    )(pos, *pieces, *powered)
+def orthonormal(powered, inverse):
+    return pl.pallas_call(
+        orthonormal_kernel,
+        out_shape=(jax.ShapeDtypeStruct((ROWS, RANK), BF16),) * 2,
+        in_specs=[whole()] * 5,
+        out_specs=(whole(),) * 2,
+        compiler_params=LIMIT,
+        cost_estimate=pl.CostEstimate(flops=6 * 896 * 256 * 256, bytes_accessed=2 << 20, transcendentals=0),
+        name="orthonormal",
+    )(*powered, inverse)
 
 
 def coefficients_kernel(pos_ref, p0, p1, p2, p3, inverse_ref, coeff_ref, high_ref, low_ref, square_ref):
@@ -522,10 +533,13 @@
     raw = jnp.concatenate([piece[: 2 * COEFF] for piece in pieces])
     grams = [gram] + [send_y(gram, s) for s in (1, 2, 3)]
     raws = [raw] + [send_y(raw, s) for s in (1, 2, 3)]
-    inverse, high, low = factor(pos, grams, powered)
+    inverse = factor(pos, grams)
 
     coefficients, c_high, c_low, squares = coefficients_of(pos, raws, inverse)
-    squares = squares + send_core(squares)
+    came = send_core(squares)
+    high, low = orthonormal(powered, inverse)
+    came, high, low = lax.optimization_barrier((came, high, low))
+    squares = squares + came
     came = [send_x(squares, s) for s in (1, 2, 3)]
     new_momentum = feedback(pos, summed, high, c_high)
     new_momentum, *came = lax.optimization_barrier((new_momentum, *came))

time: 113 us -> 112 us (level)
    pallas_call x1 -> x2, Pallas kernels: 9.8 us -> 9.84 us  [the longest x1 9.27 us: factor(): pl.pallas_call(factor_kernel, out_shape=jax.ShapeDtypeStruct((RANK, RANK)...]
where the time goes in v1:
time: 112 us
  starting transfers between devices  50.2 us (45%)
  waiting for transfers between devices  33.2 us (30%)
  Pallas kernels  27.3 us (24%)
    ppermute x31, starting transfers between devices, send(): return lax.ppermute(value, axis, [(i, move(i)) for i in range(size)])  50.2 us
    ppermute x31, waiting for transfers between devices, send(): return lax.ppermute(value, axis, [(i, move(i)) for i in range(size)])  33.2 us
    pallas_call x1, Pallas kernels, factor(): pl.pallas_call(factor_kernel, out_shape=jax.ShapeDtypeStruct((RANK, RANK)...  9.27 us
    pallas_call x1, Pallas kernels, power_away(): pl.pallas_call(power_away_kernel, out_shape=(jax.ShapeDtypeStruct((4 * PI...  4.39 us
    pallas_call x1, Pallas kernels, update(): pl.pallas_call(functools.partial(update_kernel, scale), out_shape=(jax.Sh...  3.54 us
    pallas_call x1, Pallas kernels, feedback(): pl.pallas_call(feedback_kernel, out_shape=jax.ShapeDtypeStruct((ROWS, COL...  2.92 us
  transfers between devices with their start and end apart: 31, of which 20 were waited for; matrix products, arithmetic and copies ran while one was open for 0% of the time, Pallas kernels for 15%

profile of v1, /device:TPU:2, one launch (start us, length us, event | category | flops | bytes accessed | tf_op | source)
XLA Modules:
  0.0 112.2 jit_solution(1972894276546443009)
XLA Ops:
  0.7 0.1 pad_add_fusion.pos_ref
  0.7 4.4 %power_away.1 = (f32[448,256]{1,0:T(8,128)S(1)}, bf16[448,1024]{1,0:T(8,128)(2,1)S(1)}, bf16[448,1024]{1,0:T(8,128)(2,1)S(1)}, f32[448,1024]{1,0:T(8,128)S(1)}, ...) custom-call(s32[4]{0:T(128)S(1)} %pad_add_fusion.pos_ref, ...), custom_call_target="tpu_custom_call" | custom-call | tf_op jit(solution)/shard_map/power_away/pallas_call | solution.py:123
  5.1 0.1 collective-permute-start
  5.2 1.0 power_own.1
  6.3 0.8 collective-permute-done
  7.1 2.3 %collective-permute-start.3 = (f32[112,256]{1,0:T(8,128)S(1)}, f32[112,256]{1,0:T(8,128)S(1)}, u32[]{:S(2)}, u32[]{:S(2)}) collective-permute-start(f32[112,256]{1,0:T(8,128)S(1)} %get-tuple-element.83), channel_id=1, source_target_pairs={{0,6},{1,7},{2,0},{3,1},{4,2},{5,3},{6,4},{7,5},{8,14},{9,15},{10,... | collective-permute-start | bytes 344072 | tf_op jit(solution)/shard_map/ppermute | solution.py:27
  9.4 3.1 %collective-permute-start.1 = (f32[112,256]{1,0:T(8,128)S(1)}, f32[112,256]{1,0:T(8,128)S(1)}, u32[]{:S(2)}, u32[]{:S(2)}) collective-permute-start(f32[112,256]{1,0:T(8,128)S(1)} %get-tuple-element.85), channel_id=1, source_target_pairs={{0,4},{1,5},{2,6},{3,7},{4,0},{5,1},{6,2},{7,3},{8,12},{9,13},{10,... | collective-permute-start | bytes 344072 | tf_op jit(solution)/shard_map/ppermute | solution.py:27
  12.5 2.9 %collective-permute-done.2 = f32[112,256]{1,0:T(8,128)S(1)} collective-permute-done((f32[112,256]{1,0:T(8,128)S(1)}, f32[112,256]{1,0:T(8,128)S(1)}, u32[]{:S(2)}, u32[]{:S(2)}) %collective-permute-start.2) | collective-permute-done | bytes 114720 | tf_op jit(solution)/shard_map/ppermute | solution.py:27
  15.5 0.4 collective-permute-done.1
  15.9 2.5 %collective-permute-start.6 = (f32[112,256]{1,0:T(8,128)S(1)}, f32[112,256]{1,0:T(8,128)S(1)}, u32[]{:S(2)}, u32[]{:S(2)}) collective-permute-start(f32[112,256]{1,0:T(8,128)S(1)} %fusion.1), channel_id=1, source_target_pairs={{0,2},{1,3},{2,4},{3,5},{4,6},{5,7},{6,0},{7,1},{8,10},{9,11},{10,... | collective-permute-start | bytes 344072 | tf_op jit(solution)/shard_map/ppermute | solution.py:27
  18.4 2.8 %collective-permute-start.5 = (f32[112,256]{1,0:T(8,128)S(1)}, f32[112,256]{1,0:T(8,128)S(1)}, u32[]{:S(2)}, u32[]{:S(2)}) collective-permute-start(f32[112,256]{1,0:T(8,128)S(1)} %fusion.1), channel_id=1, source_target_pairs={{0,4},{1,5},{2,6},{3,7},{4,0},{5,1},{6,2},{7,3},{8,12},{9,13},{10,... | collective-permute-start | bytes 344072 | tf_op jit(solution)/shard_map/ppermute | solution.py:27
  21.2 0.3 collective-permute-start.4
  21.6 1.2 %collective-permute-done.6 = f32[112,256]{1,0:T(8,128)S(1)} collective-permute-done((f32[112,256]{1,0:T(8,128)S(1)}, f32[112,256]{1,0:T(8,128)S(1)}, u32[]{:S(2)}, u32[]{:S(2)}) %collective-permute-start.6) | collective-permute-done | bytes 114720 | tf_op jit(solution)/shard_map/ppermute | solution.py:27
  22.8 2.1 %collective-permute-done.5 = f32[112,256]{1,0:T(8,128)S(1)} collective-permute-done((f32[112,256]{1,0:T(8,128)S(1)}, f32[112,256]{1,0:T(8,128)S(1)}, u32[]{:S(2)}, u32[]{:S(2)}) %collective-permute-start.5) | collective-permute-done | bytes 114720 | tf_op jit(solution)/shard_map/ppermute | solution.py:27
  24.9 1.2 %collective-permute-done.4 = f32[112,256]{1,0:T(8,128)S(1)} collective-permute-done((f32[112,256]{1,0:T(8,128)S(1)}, f32[112,256]{1,0:T(8,128)S(1)}, u32[]{:S(2)}, u32[]{:S(2)}) %collective-permute-start.4) | collective-permute-done | bytes 114720 | tf_op jit(solution)/shard_map/ppermute | solution.py:27
  26.1 0.1 collective-permute-start.7
  26.2 1.3 %project_own.1 = (bf16[448,256]{1,0:T(8,128)(2,1)S(1)}, bf16[448,256]{1,0:T(8,128)(2,1)S(1)}, f32[1024,256]{1,0:T(8,128)S(1)}, f32[256,256]{1,0:T(8,128)S(1)}) custom-call(bf16[448,1024]{1,0:T(8,128)(2,1)S(1)} %get-tuple-element.47.s_high.s0_high, bf16[448,1024]{1,0:T(8,128)(2,1)S(1)} %get-tuple-element.48.s_low.s0_low, f32[448,256]{1,0:T(8,128)S(1)} %pad_maximum_fusion.own_ref), custom_call_target="tpu_custom_call" | custom-call | flops 880803840 | bytes 4194304 | tf_op jit(solution)/shard_map/project_own/pallas_call | solution.py:183
  27.5 0.5 collective-permute-done.7.other_ref
  28.0 1.2 %project_far.1 = (bf16[448,256]{1,0:T(8,128)(2,1)S(1)}, bf16[448,256]{1,0:T(8,128)(2,1)S(1)}, f32[256,256]{1,0:T(8,128)S(1)}, f32[160,256]{1,0:T(8,128)S(1)}, f32[160,256]{1,0:T(8,128)S(1)}) custom-call(s32[4]{0:T(128)S(1)} %pad_add_fusion.pos_ref, bf16[448,1024]{1,0:T(8,128)(2,1)S(1)} %get-tuple-element.49.s_high.s1_high, ...), custom_call_target="tpu_custom_call" | custom-call | tf_op jit(solution)/shard_map/project_far/pallas_call | solution.py:229
  29.3 3.3 %collective-permute-start.9 = (f32[160,256]{1,0:T(8,128)S(1)}, f32[160,256]{1,0:T(8,128)S(1)}, u32[]{:S(2)}, u32[]{:S(2)}) collective-permute-start(f32[160,256]{1,0:T(8,128)S(1)} %get-tuple-element.61), channel_id=1, source_target_pairs={{0,192},{8,200},{16,208},{24,216},{32,224},{40,232},{48,240},{56,2... | collective-permute-start | bytes 491528 | tf_op jit(solution)/shard_map/ppermute | solution.py:27
  32.6 1.5 %project.1 = (f32[160,256]{1,0:T(8,128)S(1)}, f32[160,256]{1,0:T(8,128)S(1)}, f32[160,256]{1,0:T(8,128)S(1)}, f32[160,256]{1,0:T(8,128)S(1)}, f32[160,256]{1,0:T(8,128)S(1)}, /*index=5*/f32[160,256]{1,0:T(8,128)S(1)}) custom-call(s32[4]{0:T(128)S(1)} %pad_add_fusion.pos_ref, bf16[448,1024]{1,0:T(8,128)(2,1)S(1)} %get-tuple-element.49.s_high.s1_high, ...), custom_call_target="tpu_custom_call" | custom-call | flops 528482304 | bytes 4194304 | tf_op jit(solution)/shard_map/project/pallas_call | solution.py:256
  34.0 0.8 collective-permute-start.8
  34.9 1.4 %collective-permute-done.9 = f32[160,256]{1,0:T(8,128)S(1)} collective-permute-done((f32[160,256]{1,0:T(8,128)S(1)}, f32[160,256]{1,0:T(8,128)S(1)}, u32[]{:S(2)}, u32[]{:S(2)}) %collective-permute-start.9) | collective-permute-done | bytes 163872 | tf_op jit(solution)/shard_map/ppermute | solution.py:27
  36.3 3.8 %collective-permute-start.10 = (f32[160,256]{1,0:T(8,128)S(1)}, f32[160,256]{1,0:T(8,128)S(1)}, u32[]{:S(2)}, u32[]{:S(2)}) collective-permute-start(f32[160,256]{1,0:T(8,128)S(1)} %add.82), channel_id=1, source_target_pairs={{0,192},{8,200},{16,208},{24,216},{32,224},{40,232},{48,240},{56,2... | collective-permute-start | bytes 491528 | tf_op jit(solution)/shard_map/ppermute | solution.py:27
  40.1 0.1 collective-permute-start.11
  40.2 0.7 collective-permute-done.12
  40.9 1.4 %collective-permute-start.13 = (f32[160,256]{1,0:T(8,128)S(1)}, f32[160,256]{1,0:T(8,128)S(1)}, u32[]{:S(2)}, u32[]{:S(2)}) collective-permute-start(f32[160,256]{1,0:T(8,128)S(1)} %add.85), channel_id=1, source_target_pairs={{0,64},{8,72},{16,80},{24,88},{32,96},{40,104},{48,112},{56,120},{... | collective-permute-start | bytes 491528 | tf_op jit(solution)/shard_map/ppermute | solution.py:27
  42.2 1.0 collective-permute-done.8
  43.3 1.5 %collective-permute-done.10 = f32[160,256]{1,0:T(8,128)S(1)} collective-permute-done((f32[160,256]{1,0:T(8,128)S(1)}, f32[160,256]{1,0:T(8,128)S(1)}, u32[]{:S(2)}, u32[]{:S(2)}) %collective-permute-start.10) | collective-permute-done | bytes 163872 | tf_op jit(solution)/shard_map/ppermute | solution.py:27
  44.8 5.9 %collective-permute-start.16 = (f32[80,256]{1,0:T(8,128)S(1)}, f32[80,256]{1,0:T(8,128)S(1)}, u32[]{:S(2)}, u32[]{:S(2)}) collective-permute-start(f32[80,256]{1,0:T(8,128)S(1)} %slice.87), channel_id=1, source_target_pairs={{0,56},{8,0},{16,8},{24,16},{32,24},{40,32},{48,40},{56,48},{64,12... | collective-permute-start | bytes 245768 | tf_op jit(solution)/shard_map/ppermute | solution.py:27
  50.8 0.1 collective-permute-start.15
  50.9 1.9 %collective-permute-start.14 = (f32[80,256]{1,0:T(8,128)S(1)}, f32[80,256]{1,0:T(8,128)S(1)}, u32[]{:S(2)}, u32[]{:S(2)}) collective-permute-start(f32[80,256]{1,0:T(8,128)S(1)} %get-tuple-element.87), channel_id=1, source_target_pairs={{0,16},{8,24},{16,32},{24,40},{32,48},{40,56},{48,0},{56,8},{64,80... | collective-permute-start | bytes 245768 | tf_op jit(solution)/shard_map/ppermute | solution.py:27
  52.8 0.0 collective-permute-done.16
  52.8 3.7 %collective-permute-done.15 = f32[80,256]{1,0:T(8,128)S(1)} collective-permute-done((f32[80,256]{1,0:T(8,128)S(1)}, f32[80,256]{1,0:T(8,128)S(1)}, u32[]{:S(2)}, u32[]{:S(2)}) %collective-permute-start.15) | collective-permute-done | bytes 81952 | tf_op jit(solution)/shard_map/ppermute | solution.py:27
  56.5 2.6 %collective-permute-done.14 = f32[80,256]{1,0:T(8,128)S(1)} collective-permute-done((f32[80,256]{1,0:T(8,128)S(1)}, f32[80,256]{1,0:T(8,128)S(1)}, u32[]{:S(2)}, u32[]{:S(2)}) %collective-permute-start.14) | collective-permute-done | bytes 81952 | tf_op jit(solution)/shard_map/ppermute | solution.py:27
  59.1 4.4 %collective-permute-start.17 = (f32[80,256]{1,0:T(8,128)S(1)}, f32[80,256]{1,0:T(8,128)S(1)}, u32[]{:S(2)}, u32[]{:S(2)}) collective-permute-start(f32[80,256]{1,0:T(8,128)S(1)} %fusion.2), channel_id=1, source_target_pairs={{0,32},{8,40},{16,48},{24,56},{32,0},{40,8},{48,16},{56,24},{64,96... | collective-permute-start | bytes 245768 | tf_op jit(solution)/shard_map/ppermute | solution.py:27
  63.5 4.9 %collective-permute-done.17 = f32[80,256]{1,0:T(8,128)S(1)} collective-permute-done((f32[80,256]{1,0:T(8,128)S(1)}, f32[80,256]{1,0:T(8,128)S(1)}, u32[]{:S(2)}, u32[]{:S(2)}) %collective-permute-start.17) | collective-permute-done | bytes 81952 | tf_op jit(solution)/shard_map/ppermute | solution.py:27
  68.5 0.1 collective-permute-start.20
  68.5 0.5 collective-permute-start.19
  69.1 1.5 %collective-permute-start.18 = (f32[80,256]{1,0:T(8,128)S(1)}, f32[80,256]{1,0:T(8,128)S(1)}, u32[]{:S(2)}, u32[]{:S(2)}) collective-permute-start(f32[80,256]{1,0:T(8,128)S(1)} %add.90), channel_id=1, source_target_pairs={{0,8},{8,16},{16,24},{24,32},{32,40},{40,48},{48,56},{56,0},{64,72... | collective-permute-start | bytes 245768 | tf_op jit(solution)/shard_map/ppermute | solution.py:27
  70.6 2.4 %collective-permute-done.20 = f32[80,256]{1,0:T(8,128)S(1)} collective-permute-done((f32[80,256]{1,0:T(8,128)S(1)}, f32[80,256]{1,0:T(8,128)S(1)}, u32[]{:S(2)}, u32[]{:S(2)}) %collective-permute-start.20) | collective-permute-done | bytes 81952 | tf_op jit(solution)/shard_map/ppermute | solution.py:27
  73.0 3.1 %collective-permute-done.19 = f32[80,256]{1,0:T(8,128)S(1)} collective-permute-done((f32[80,256]{1,0:T(8,128)S(1)}, f32[80,256]{1,0:T(8,128)S(1)}, u32[]{:S(2)}, u32[]{:S(2)}) %collective-permute-start.19) | collective-permute-done | bytes 81952 | tf_op jit(solution)/shard_map/ppermute | solution.py:27
  76.1 0.9 collective-permute-done.18
  76.9 4.1 %collective-permute-start.26 = (f32[64,256]{1,0:T(8,128)S(1)}, f32[64,256]{1,0:T(8,128)S(1)}, u32[]{:S(2)}, u32[]{:S(2)}) collective-permute-start(f32[64,256]{1,0:T(8,128)S(1)} %pad_maximum_fusion.2.p0), channel_id=1, source_target_pairs={{0,192},{8,200},{16,208},{24,216},{32,224},{40,232},{48,240},{56,2... | collective-permute-start | bytes 196616 | tf_op jit(solution)/shard_map/ppermute | solution.py:27
  81.0 0.0 collective-permute-start.25
  81.0 1.0 collective-permute-start.24
  82.0 2.4 %collective-permute-start.23 = (f32[256,256]{1,0:T(8,128)S(1)}, f32[256,256]{1,0:T(8,128)S(1)}, u32[]{:S(2)}, u32[]{:S(2)}) collective-permute-start(f32[256,256]{1,0:T(8,128)S(1)} %pad_maximum_fusion.1.p0), channel_id=1, source_target_pairs={{0,192},{8,200},{16,208},{24,216},{32,224},{40,232},{48,240},{56,2... | collective-permute-start | bytes 786440 | tf_op jit(solution)/shard_map/ppermute | solution.py:27
  84.4 2.3 %collective-permute-start.22 = (f32[256,256]{1,0:T(8,128)S(1)}, f32[256,256]{1,0:T(8,128)S(1)}, u32[]{:S(2)}, u32[]{:S(2)}) collective-permute-start(f32[256,256]{1,0:T(8,128)S(1)} %pad_maximum_fusion.1.p0), channel_id=1, source_target_pairs={{0,128},{8,136},{16,144},{24,152},{32,160},{40,168},{48,176},{56,1... | collective-permute-start | bytes 786440 | tf_op jit(solution)/shard_map/ppermute | solution.py:27
  86.7 0.0 collective-permute-done.26.p3
  86.7 0.0 collective-permute-start.21
  86.7 0.8 collective-permute-done.25.p2
  87.6 0.4 collective-permute-done.24.p1
  88.0 9.3 %factor.1.inverse_ref = f32[256,256]{1,0:T(8,128)S(1)} custom-call(s32[4]{0:T(128)S(1)} %pad_add_fusion.pos_ref, f32[64,256]{1,0:T(8,128)S(1)} %pad_maximum_fusion.2.p0, f32[64,256]{1,0:T(8,128)S(1)} %collective-permute-done.24.p1, f32[64,256]{1,0:T(8,128)S(1)} %collective-permute-done.25.p2, f32[64,256]{1,0:T(8,128)S(1)} %collective-permute-done.26.p3), custom_call_target="tpu_custom_call" | custom-call | flops 10737418240 | bytes 33554432 | tf_op jit(solution)/shard_map/factor/pallas_call | solution.py:366
  97.3 0.0 collective-permute-done.22.p2
  97.3 0.0 collective-permute-done.21.p1
  97.3 1.6 %coefficients.1 = (f32[1024,256]{1,0:T(8,128)S(1)}, bf16[1024,256]{1,0:T(8,128)(2,1)S(1)}, bf16[1024,256]{1,0:T(8,128)(2,1)S(1)}, f32[1,256]{1,0:T(1,128)S(1)}) custom-call(s32[4]{0:T(128)S(1)} %pad_add_fusion.pos_ref, f32[256,256]{1,0:T(8,128)S(1)} %pad_maximum_fusion.1.p0, f32[256,256]{1,0:T(8,128)S(1)} %collective-permute-done.21.p1, ...), custom_call_target="tpu_custom_call" | custom-call | tf_op jit(solution)/shard_map/coefficients/pallas_call | solution.py:412
  98.9 0.1 collective-permute-start.27
  99.0 0.6 orthonormal.1
  99.6 0.6 collective-permute-done.27
  100.1 1.6 %collective-permute-start.30 = (f32[1,256]{1,0:T(1,128)S(1)}, f32[1,256]{1,0:T(1,128)S(1)}, u32[]{:S(2)}, u32[]{:S(2)}) collective-permute-start(f32[1,256]{1,0:T(1,128)S(1)} %add.91), channel_id=1, source_target_pairs={{0,6},{1,7},{2,0},{3,1},{4,2},{5,3},{6,4},{7,5},{8,14},{9,15},{10,... | collective-permute-start | bytes 3080 | tf_op jit(solution)/shard_map/ppermute | solution.py:27
  101.7 1.2 %collective-permute-start.29 = (f32[1,256]{1,0:T(1,128)S(1)}, f32[1,256]{1,0:T(1,128)S(1)}, u32[]{:S(2)}, u32[]{:S(2)}) collective-permute-start(f32[1,256]{1,0:T(1,128)S(1)} %add.91), channel_id=1, source_target_pairs={{0,4},{1,5},{2,6},{3,7},{4,0},{5,1},{6,2},{7,3},{8,12},{9,13},{10,... | collective-permute-start | bytes 3080 | tf_op jit(solution)/shard_map/ppermute | solution.py:27
  102.9 2.6 %collective-permute-start.28 = (f32[1,256]{1,0:T(1,128)S(1)}, f32[1,256]{1,0:T(1,128)S(1)}, u32[]{:S(2)}, u32[]{:S(2)}) collective-permute-start(f32[1,256]{1,0:T(1,128)S(1)} %add.91), channel_id=1, source_target_pairs={{0,2},{1,3},{2,4},{3,5},{4,6},{5,7},{6,0},{7,1},{8,10},{9,11},{10,... | collective-permute-start | bytes 3080 | tf_op jit(solution)/shard_map/ppermute | solution.py:27
  105.5 2.9 %feedback.1 = f32[896,1024]{1,0:T(8,128)} custom-call(s32[4]{0:T(128)S(1)} %pad_add_fusion.pos_ref, bf16[448,1024]{1,0:T(8,128)(2,1)S(1)} %get-tuple-element.47.s_high.s0_high, bf16[448,1024]{1,0:T(8,128)(2,1)S(1)} %get-tuple-element.48.s_low.s0_low, bf16[448,1024]{1,0:T(8,128)(2,1)S(1)} %get-tuple-element.49.s_high.s1_high, ...), custom_call_target="tpu_custom_call" | custom-call | flops 939524096 | bytes 10485760 | tf_op jit(solution)/shard_map/feedback/pallas_call | solution.py:451
  108.5 3.5 %update.1 = (f32[1024,256]{1,0:T(8,128)}, bf16[896,1024]{1,0:T(8,128)(2,1)}) custom-call(s32[4]{0:T(128)S(1)} %pad_add_fusion.pos_ref, bf16[896,256]{1,0:T(8,128)(2,1)S(1)} %get-tuple-element.71.q_ref.high_ref, bf16[896,256]{1,0:T(8,128)(2,1)S(1)} %get-tuple-element.75.low_ref, f32[1024,256]{1,0:T(8,128)S(1)} %get-tuple-element.76.c_ref, ...), custom_call_target="tpu_custom_call" | custom-call | tf_op jit(solution)/shard_map/update/pallas_call | solution.py:483
  (32 shorter events, 0.4 us)
Async XLA Ops:
  5.1 1.9 %collective-permute-start = (f32[448,256]{1,0:T(8,128)S(1)}, f32[448,256]{1,0:T(8,128)S(1)}, u32[]{:S(2)}, u32[]{:S(2)}) collective-permute-start(f32[448,256]{1,0:T(8,128)S(1)} %get-tuple-element.52), channel_id=1, source_target_pairs={{0,1},{1,0},{2,3},{3,2},{4,5},{5,4},{6,7},{7,6},{8,9},{9,8},{10,11... | collective-permute-start | bytes 1376264 | tf_op jit(solution)/shard_map/ppermute | solution.py:27
  7.1 5.4 %collective-permute-start.3 = (f32[112,256]{1,0:T(8,128)S(1)}, f32[112,256]{1,0:T(8,128)S(1)}, u32[]{:S(2)}, u32[]{:S(2)}) collective-permute-start(f32[112,256]{1,0:T(8,128)S(1)} %get-tuple-element.83), channel_id=1, source_target_pairs={{0,6},{1,7},{2,0},{3,1},{4,2},{5,3},{6,4},{7,5},{8,14},{9,15},{10,... | collective-permute-start | bytes 344072 | tf_op jit(solution)/shard_map/ppermute | solution.py:27
  9.4 6.0 %collective-permute-start.2 = (f32[112,256]{1,0:T(8,128)S(1)}, f32[112,256]{1,0:T(8,128)S(1)}, u32[]{:S(2)}, u32[]{:S(2)}) collective-permute-start(f32[112,256]{1,0:T(8,128)S(1)} %get-tuple-element.84), channel_id=1, source_target_pairs={{0,2},{1,3},{2,4},{3,5},{4,6},{5,7},{6,0},{7,1},{8,10},{9,11},{10,... | collective-permute-start | bytes 344072 | tf_op jit(solution)/shard_map/ppermute | solution.py:27
  9.4 6.4 %collective-permute-start.1 = (f32[112,256]{1,0:T(8,128)S(1)}, f32[112,256]{1,0:T(8,128)S(1)}, u32[]{:S(2)}, u32[]{:S(2)}) collective-permute-start(f32[112,256]{1,0:T(8,128)S(1)} %get-tuple-element.85), channel_id=1, source_target_pairs={{0,4},{1,5},{2,6},{3,7},{4,0},{5,1},{6,2},{7,3},{8,12},{9,13},{10,... | collective-permute-start | bytes 344072 | tf_op jit(solution)/shard_map/ppermute | solution.py:27
  15.9 6.9 %collective-permute-start.6 = (f32[112,256]{1,0:T(8,128)S(1)}, f32[112,256]{1,0:T(8,128)S(1)}, u32[]{:S(2)}, u32[]{:S(2)}) collective-permute-start(f32[112,256]{1,0:T(8,128)S(1)} %fusion.1), channel_id=1, source_target_pairs={{0,2},{1,3},{2,4},{3,5},{4,6},{5,7},{6,0},{7,1},{8,10},{9,11},{10,... | collective-permute-start | bytes 344072 | tf_op jit(solution)/shard_map/ppermute | solution.py:27
  18.4 6.5 %collective-permute-start.5 = (f32[112,256]{1,0:T(8,128)S(1)}, f32[112,256]{1,0:T(8,128)S(1)}, u32[]{:S(2)}, u32[]{:S(2)}) collective-permute-start(f32[112,256]{1,0:T(8,128)S(1)} %fusion.1), channel_id=1, source_target_pairs={{0,4},{1,5},{2,6},{3,7},{4,0},{5,1},{6,2},{7,3},{8,12},{9,13},{10,... | collective-permute-start | bytes 344072 | tf_op jit(solution)/shard_map/ppermute | solution.py:27
  21.2 4.9 %collective-permute-start.4 = (f32[112,256]{1,0:T(8,128)S(1)}, f32[112,256]{1,0:T(8,128)S(1)}, u32[]{:S(2)}, u32[]{:S(2)}) collective-permute-start(f32[112,256]{1,0:T(8,128)S(1)} %fusion.1), channel_id=1, source_target_pairs={{0,6},{1,7},{2,0},{3,1},{4,2},{5,3},{6,4},{7,5},{8,14},{9,15},{10,... | collective-permute-start | bytes 344072 | tf_op jit(solution)/shard_map/ppermute | solution.py:27
  26.1 1.9 %collective-permute-start.7 = (f32[448,256]{1,0:T(8,128)S(1)}, f32[448,256]{1,0:T(8,128)S(1)}, u32[]{:S(2)}, u32[]{:S(2)}) collective-permute-start(f32[448,256]{1,0:T(8,128)S(1)} %pad_maximum_fusion.own_ref), channel_id=1, source_target_pairs={{0,1},{1,0},{2,3},{3,2},{4,5},{5,4},{6,7},{7,6},{8,9},{9,8},{10,11... | collective-permute-start | bytes 1376264 | tf_op jit(solution)/shard_map/ppermute | solution.py:27
  29.3 7.0 %collective-permute-start.9 = (f32[160,256]{1,0:T(8,128)S(1)}, f32[160,256]{1,0:T(8,128)S(1)}, u32[]{:S(2)}, u32[]{:S(2)}) collective-permute-start(f32[160,256]{1,0:T(8,128)S(1)} %get-tuple-element.61), channel_id=1, source_target_pairs={{0,192},{8,200},{16,208},{24,216},{32,224},{40,232},{48,240},{56,2... | collective-permute-start | bytes 491528 | tf_op jit(solution)/shard_map/ppermute | solution.py:27
  32.6 8.3 %collective-permute-start.12 = (f32[160,256]{1,0:T(8,128)S(1)}, f32[160,256]{1,0:T(8,128)S(1)}, u32[]{:S(2)}, u32[]{:S(2)}) collective-permute-start(f32[160,256]{1,0:T(8,128)S(1)} %get-tuple-element.65), channel_id=1, source_target_pairs={{0,64},{8,72},{16,80},{24,88},{32,96},{40,104},{48,112},{56,120},{... | collective-permute-start | bytes 491528 | tf_op jit(solution)/shard_map/ppermute | solution.py:27
  34.0 9.2 %collective-permute-start.8 = (f32[160,256]{1,0:T(8,128)S(1)}, f32[160,256]{1,0:T(8,128)S(1)}, u32[]{:S(2)}, u32[]{:S(2)}) collective-permute-start(f32[160,256]{1,0:T(8,128)S(1)} %get-tuple-element.59), channel_id=1, source_target_pairs={{0,64},{8,72},{16,80},{24,88},{32,96},{40,104},{48,112},{56,120},{... | collective-permute-start | bytes 491528 | tf_op jit(solution)/shard_map/ppermute | solution.py:27
  36.3 8.4 %collective-permute-start.10 = (f32[160,256]{1,0:T(8,128)S(1)}, f32[160,256]{1,0:T(8,128)S(1)}, u32[]{:S(2)}, u32[]{:S(2)}) collective-permute-start(f32[160,256]{1,0:T(8,128)S(1)} %add.82), channel_id=1, source_target_pairs={{0,192},{8,200},{16,208},{24,216},{32,224},{40,232},{48,240},{56,2... | collective-permute-start | bytes 491528 | tf_op jit(solution)/shard_map/ppermute | solution.py:27
  40.1 10.6 %collective-permute-start.11 = (f32[160,256]{1,0:T(8,128)S(1)}, f32[160,256]{1,0:T(8,128)S(1)}, u32[]{:S(2)}, u32[]{:S(2)}) collective-permute-start(f32[160,256]{1,0:T(8,128)S(1)} %get-tuple-element.63), channel_id=1, source_target_pairs={{0,192},{8,200},{16,208},{24,216},{32,224},{40,232},{48,240},{56,2... | collective-permute-start | bytes 491528 | tf_op jit(solution)/shard_map/ppermute | solution.py:27
  40.9 9.9 %collective-permute-start.13 = (f32[160,256]{1,0:T(8,128)S(1)}, f32[160,256]{1,0:T(8,128)S(1)}, u32[]{:S(2)}, u32[]{:S(2)}) collective-permute-start(f32[160,256]{1,0:T(8,128)S(1)} %add.85), channel_id=1, source_target_pairs={{0,64},{8,72},{16,80},{24,88},{32,96},{40,104},{48,112},{56,120},{... | collective-permute-start | bytes 491528 | tf_op jit(solution)/shard_map/ppermute | solution.py:27
  44.8 8.0 %collective-permute-start.16 = (f32[80,256]{1,0:T(8,128)S(1)}, f32[80,256]{1,0:T(8,128)S(1)}, u32[]{:S(2)}, u32[]{:S(2)}) collective-permute-start(f32[80,256]{1,0:T(8,128)S(1)} %slice.87), channel_id=1, source_target_pairs={{0,56},{8,0},{16,8},{24,16},{32,24},{40,32},{48,40},{56,48},{64,12... | collective-permute-start | bytes 245768 | tf_op jit(solution)/shard_map/ppermute | solution.py:27
  50.8 5.7 %collective-permute-start.15 = (f32[80,256]{1,0:T(8,128)S(1)}, f32[80,256]{1,0:T(8,128)S(1)}, u32[]{:S(2)}, u32[]{:S(2)}) collective-permute-start(f32[80,256]{1,0:T(8,128)S(1)} %get-tuple-element.86), channel_id=1, source_target_pairs={{0,8},{8,16},{16,24},{24,32},{32,40},{40,48},{48,56},{56,0},{64,72... | collective-permute-start | bytes 245768 | tf_op jit(solution)/shard_map/ppermute | solution.py:27
  50.9 8.2 %collective-permute-start.14 = (f32[80,256]{1,0:T(8,128)S(1)}, f32[80,256]{1,0:T(8,128)S(1)}, u32[]{:S(2)}, u32[]{:S(2)}) collective-permute-start(f32[80,256]{1,0:T(8,128)S(1)} %get-tuple-element.87), channel_id=1, source_target_pairs={{0,16},{8,24},{16,32},{24,40},{32,48},{40,56},{48,0},{56,8},{64,80... | collective-permute-start | bytes 245768 | tf_op jit(solution)/shard_map/ppermute | solution.py:27
  59.1 9.3 %collective-permute-start.17 = (f32[80,256]{1,0:T(8,128)S(1)}, f32[80,256]{1,0:T(8,128)S(1)}, u32[]{:S(2)}, u32[]{:S(2)}) collective-permute-start(f32[80,256]{1,0:T(8,128)S(1)} %fusion.2), channel_id=1, source_target_pairs={{0,32},{8,40},{16,48},{24,56},{32,0},{40,8},{48,16},{56,24},{64,96... | collective-permute-start | bytes 245768 | tf_op jit(solution)/shard_map/ppermute | solution.py:27
  68.5 4.5 %collective-permute-start.20 = (f32[80,256]{1,0:T(8,128)S(1)}, f32[80,256]{1,0:T(8,128)S(1)}, u32[]{:S(2)}, u32[]{:S(2)}) collective-permute-start(f32[80,256]{1,0:T(8,128)S(1)} %add.90), channel_id=1, source_target_pairs={{0,56},{8,0},{16,8},{24,16},{32,24},{40,32},{48,40},{56,48},{64,12... | collective-permute-start | bytes 245768 | tf_op jit(solution)/shard_map/ppermute | solution.py:27
  68.5 7.5 %collective-permute-start.19 = (f32[80,256]{1,0:T(8,128)S(1)}, f32[80,256]{1,0:T(8,128)S(1)}, u32[]{:S(2)}, u32[]{:S(2)}) collective-permute-start(f32[80,256]{1,0:T(8,128)S(1)} %add.90), channel_id=1, source_target_pairs={{0,16},{8,24},{16,32},{24,40},{32,48},{40,56},{48,0},{56,8},{64,80... | collective-permute-start | bytes 245768 | tf_op jit(solution)/shard_map/ppermute | solution.py:27
  69.1 7.9 %collective-permute-start.18 = (f32[80,256]{1,0:T(8,128)S(1)}, f32[80,256]{1,0:T(8,128)S(1)}, u32[]{:S(2)}, u32[]{:S(2)}) collective-permute-start(f32[80,256]{1,0:T(8,128)S(1)} %add.90), channel_id=1, source_target_pairs={{0,8},{8,16},{16,24},{24,32},{32,40},{40,48},{48,56},{56,0},{64,72... | collective-permute-start | bytes 245768 | tf_op jit(solution)/shard_map/ppermute | solution.py:27
  76.9 9.8 %collective-permute-start.26 = (f32[64,256]{1,0:T(8,128)S(1)}, f32[64,256]{1,0:T(8,128)S(1)}, u32[]{:S(2)}, u32[]{:S(2)}) collective-permute-start(f32[64,256]{1,0:T(8,128)S(1)} %pad_maximum_fusion.2.p0), channel_id=1, source_target_pairs={{0,192},{8,200},{16,208},{24,216},{32,224},{40,232},{48,240},{56,2... | collective-permute-start | bytes 196616 | tf_op jit(solution)/shard_map/ppermute | solution.py:27
  81.0 6.5 %collective-permute-start.25 = (f32[64,256]{1,0:T(8,128)S(1)}, f32[64,256]{1,0:T(8,128)S(1)}, u32[]{:S(2)}, u32[]{:S(2)}) collective-permute-start(f32[64,256]{1,0:T(8,128)S(1)} %pad_maximum_fusion.2.p0), channel_id=1, source_target_pairs={{0,128},{8,136},{16,144},{24,152},{32,160},{40,168},{48,176},{56,1... | collective-permute-start | bytes 196616 | tf_op jit(solution)/shard_map/ppermute | solution.py:27
  81.0 6.9 %collective-permute-start.24 = (f32[64,256]{1,0:T(8,128)S(1)}, f32[64,256]{1,0:T(8,128)S(1)}, u32[]{:S(2)}, u32[]{:S(2)}) collective-permute-start(f32[64,256]{1,0:T(8,128)S(1)} %pad_maximum_fusion.2.p0), channel_id=1, source_target_pairs={{0,64},{8,72},{16,80},{24,88},{32,96},{40,104},{48,112},{56,120},{... | collective-permute-start | bytes 196616 | tf_op jit(solution)/shard_map/ppermute | solution.py:27
  82.0 15.2 %collective-permute-start.23 = (f32[256,256]{1,0:T(8,128)S(1)}, f32[256,256]{1,0:T(8,128)S(1)}, u32[]{:S(2)}, u32[]{:S(2)}) collective-permute-start(f32[256,256]{1,0:T(8,128)S(1)} %pad_maximum_fusion.1.p0), channel_id=1, source_target_pairs={{0,192},{8,200},{16,208},{24,216},{32,224},{40,232},{48,240},{56,2... | collective-permute-start | bytes 786440 | tf_op jit(solution)/shard_map/ppermute | solution.py:27
  84.4 12.9 %collective-permute-start.22 = (f32[256,256]{1,0:T(8,128)S(1)}, f32[256,256]{1,0:T(8,128)S(1)}, u32[]{:S(2)}, u32[]{:S(2)}) collective-permute-start(f32[256,256]{1,0:T(8,128)S(1)} %pad_maximum_fusion.1.p0), channel_id=1, source_target_pairs={{0,128},{8,136},{16,144},{24,152},{32,160},{40,168},{48,176},{56,1... | collective-permute-start | bytes 786440 | tf_op jit(solution)/shard_map/ppermute | solution.py:27
  86.7 10.6 %collective-permute-start.21 = (f32[256,256]{1,0:T(8,128)S(1)}, f32[256,256]{1,0:T(8,128)S(1)}, u32[]{:S(2)}, u32[]{:S(2)}) collective-permute-start(f32[256,256]{1,0:T(8,128)S(1)} %pad_maximum_fusion.1.p0), channel_id=1, source_target_pairs={{0,64},{8,72},{16,80},{24,88},{32,96},{40,104},{48,112},{56,120},{... | collective-permute-start | bytes 786440 | tf_op jit(solution)/shard_map/ppermute | solution.py:27
  98.9 1.2 %collective-permute-start.27 = (f32[1,256]{1,0:T(1,128)S(1)}, f32[1,256]{1,0:T(1,128)S(1)}, u32[]{:S(2)}, u32[]{:S(2)}) collective-permute-start(f32[1,256]{1,0:T(1,128)S(1)} %get-tuple-element.66), channel_id=1, source_target_pairs={{0,1},{1,0},{2,3},{3,2},{4,5},{5,4},{6,7},{7,6},{8,9},{9,8},{10,11... | collective-permute-start | bytes 3080 | tf_op jit(solution)/shard_map/ppermute | solution.py:27
  100.1 8.3 %collective-permute-start.30 = (f32[1,256]{1,0:T(1,128)S(1)}, f32[1,256]{1,0:T(1,128)S(1)}, u32[]{:S(2)}, u32[]{:S(2)}) collective-permute-start(f32[1,256]{1,0:T(1,128)S(1)} %add.91), channel_id=1, source_target_pairs={{0,6},{1,7},{2,0},{3,1},{4,2},{5,3},{6,4},{7,5},{8,14},{9,15},{10,... | collective-permute-start | bytes 3080 | tf_op jit(solution)/shard_map/ppermute | solution.py:27
  101.7 6.7 %collective-permute-start.29 = (f32[1,256]{1,0:T(1,128)S(1)}, f32[1,256]{1,0:T(1,128)S(1)}, u32[]{:S(2)}, u32[]{:S(2)}) collective-permute-start(f32[1,256]{1,0:T(1,128)S(1)} %add.91), channel_id=1, source_target_pairs={{0,4},{1,5},{2,6},{3,7},{4,0},{5,1},{6,2},{7,3},{8,12},{9,13},{10,... | collective-permute-start | bytes 3080 | tf_op jit(solution)/shard_map/ppermute | solution.py:27
  102.9 5.6 %collective-permute-start.28 = (f32[1,256]{1,0:T(1,128)S(1)}, f32[1,256]{1,0:T(1,128)S(1)}, u32[]{:S(2)}, u32[]{:S(2)}) collective-permute-start(f32[1,256]{1,0:T(1,128)S(1)} %add.91), channel_id=1, source_target_pairs={{0,2},{1,3},{2,4},{3,5},{4,6},{5,7},{6,0},{7,1},{8,10},{9,11},{10,... | collective-permute-start | bytes 3080 | tf_op jit(solution)/shard_map/ppermute | solution.py:27

commit v2 on v1

--- a/solution.py
+++ b/solution.py
@@ -375,26 +375,27 @@
     )(pos, *pieces)
 
 
-def orthonormal_kernel(p0_high, p0_low, p1_high, p1_low, inverse_ref, high_ref, low_ref):
+def orthonormal_kernel(p0_high, p0_low, p1_high, p1_low, inverse_ref, c_ref, high_ref, low_ref, c_high, c_low):
+    c_high[...], c_low[...] = split(c_ref[...])
     inverse = split(inverse_ref[...])
     for t, (p_high, p_low) in enumerate(((p0_high, p0_low), (p1_high, p1_low))):
         rows = pl.ds(t * 4 * PIECE, 4 * PIECE)
         high_ref[rows], low_ref[rows] = split(mm3((p_high[...], p_low[...]), inverse, 1, 1))
 
 
-def orthonormal(powered, inverse):
+def orthonormal(powered, inverse, coefficients):
     return pl.pallas_call(
         orthonormal_kernel,
-        out_shape=(jax.ShapeDtypeStruct((ROWS, RANK), BF16),) * 2,
-        in_specs=[whole()] * 5,
-        out_specs=(whole(),) * 2,
+        out_shape=(jax.ShapeDtypeStruct((ROWS, RANK), BF16),) * 2 + (jax.ShapeDtypeStruct((COLS, RANK), BF16),) * 2,
+        in_specs=[whole()] * 6,
+        out_specs=(whole(),) * 4,
         compiler_params=LIMIT,
         cost_estimate=pl.CostEstimate(flops=6 * 896 * 256 * 256, bytes_accessed=2 << 20, transcendentals=0),
         name="orthonormal",
-    )(*powered, inverse)
-
-
-def coefficients_kernel(pos_ref, p0, p1, p2, p3, inverse_ref, coeff_ref, high_ref, low_ref, square_ref):
+    )(*powered, inverse, coefficients)
+
+
+def coefficients_kernel(pos_ref, p0, p1, p2, p3, inverse_ref, coeff_ref, square_ref):
     y, z = pos_ref[0], pos_ref[1]
     inverse = split(inverse_ref[...])
     for j, piece in enumerate((p0, p1, p2, p3)):
@@ -404,7 +405,6 @@
                 place = pl.ds(pl.multiple_of(owner(y, z, j, a, b) * COEFF, COEFF), COEFF)
                 coeff_ref[place, :] = value[(2 * a + b) * COEFF : (2 * a + b + 1) * COEFF]
     value = coeff_ref[...]
-    high_ref[...], low_ref[...] = split(value)
     square_ref[...] = jnp.sum(value * value, axis=0, keepdims=True)
 
 
@@ -413,12 +413,10 @@
         coefficients_kernel,
         out_shape=(
             jax.ShapeDtypeStruct((COLS, RANK), F32),
-            jax.ShapeDtypeStruct((COLS, RANK), BF16),
-            jax.ShapeDtypeStruct((COLS, RANK), BF16),
             jax.ShapeDtypeStruct((1, RANK), F32),
         ),
         in_specs=[scalars()] + [whole()] * 5,
-        out_specs=(whole(),) * 4,
+        out_specs=(whole(),) * 2,
         compiler_params=LIMIT,
         name="coefficients",
     )(pos, *pieces, inverse)
@@ -535,9 +533,9 @@
     raws = [raw] + [send_y(raw, s) for s in (1, 2, 3)]
     inverse = factor(pos, grams)
 
-    coefficients, c_high, c_low, squares = coefficients_of(pos, raws, inverse)
+    coefficients, squares = coefficients_of(pos, raws, inverse)
     came = send_core(squares)
-    high, low = orthonormal(powered, inverse)
+    high, low, c_high, c_low = orthonormal(powered, inverse, coefficients)
     came, high, low = lax.optimization_barrier((came, high, low))
     squares = squares + came
     came = [send_x(squares, s) for s in (1, 2, 3)]

time: 112 us -> 112 us (level)
  no operation moved by 1% of the time
where the time goes in v2:
time: 112 us
  starting transfers between devices  50.2 us (45%)
  waiting for transfers between devices  32.9 us (29%)
  Pallas kernels  27.3 us (24%)
    ppermute x31, starting transfers between devices, send(): return lax.ppermute(value, axis, [(i, move(i)) for i in range(size)])  50.2 us
    ppermute x31, waiting for transfers between devices, send(): return lax.ppermute(value, axis, [(i, move(i)) for i in range(size)])  32.9 us
    pallas_call x1, Pallas kernels, factor(): pl.pallas_call(factor_kernel, out_shape=jax.ShapeDtypeStruct((RANK, RANK)...  9.28 us
    pallas_call x1, Pallas kernels, power_away(): pl.pallas_call(power_away_kernel, out_shape=(jax.ShapeDtypeStruct((4 * PI...  4.39 us
    pallas_call x1, Pallas kernels, update(): pl.pallas_call(functools.partial(update_kernel, scale), out_shape=(jax.Sh...  3.53 us
    pallas_call x1, Pallas kernels, feedback(): pl.pallas_call(feedback_kernel, out_shape=jax.ShapeDtypeStruct((ROWS, COL...  2.94 us
  transfers between devices with their start and end apart: 31, of which 20 were waited for; matrix products, arithmetic and copies ran while one was open for 0% of the time, Pallas kernels for 15%

profile of v2, /device:TPU:2, one launch (start us, length us, event | category | flops | bytes accessed | tf_op | source)
XLA Modules:
  0.0 111.9 jit_solution(4606134204398849706)
XLA Ops:
  0.7 0.1 pad_add_fusion.pos_ref
  0.7 4.4 %power_away.1 = (f32[448,256]{1,0:T(8,128)S(1)}, bf16[448,1024]{1,0:T(8,128)(2,1)S(1)}, bf16[448,1024]{1,0:T(8,128)(2,1)S(1)}, f32[448,1024]{1,0:T(8,128)S(1)}, ...) custom-call(s32[4]{0:T(128)S(1)} %pad_add_fusion.pos_ref, ...), custom_call_target="tpu_custom_call" | custom-call | tf_op jit(solution)/shard_map/power_away/pallas_call | solution.py:123
  5.1 0.1 collective-permute-start
  5.2 1.0 power_own.1
  6.3 0.8 collective-permute-done
  7.1 2.3 %collective-permute-start.3 = (f32[112,256]{1,0:T(8,128)S(1)}, f32[112,256]{1,0:T(8,128)S(1)}, u32[]{:S(2)}, u32[]{:S(2)}) collective-permute-start(f32[112,256]{1,0:T(8,128)S(1)} %get-tuple-element.83), channel_id=1, source_target_pairs={{0,6},{1,7},{2,0},{3,1},{4,2},{5,3},{6,4},{7,5},{8,14},{9,15},{10,... | collective-permute-start | bytes 344072 | tf_op jit(solution)/shard_map/ppermute | solution.py:27
  9.4 3.1 %collective-permute-start.1 = (f32[112,256]{1,0:T(8,128)S(1)}, f32[112,256]{1,0:T(8,128)S(1)}, u32[]{:S(2)}, u32[]{:S(2)}) collective-permute-start(f32[112,256]{1,0:T(8,128)S(1)} %get-tuple-element.85), channel_id=1, source_target_pairs={{0,4},{1,5},{2,6},{3,7},{4,0},{5,1},{6,2},{7,3},{8,12},{9,13},{10,... | collective-permute-start | bytes 344072 | tf_op jit(solution)/shard_map/ppermute | solution.py:27
  12.5 2.9 %collective-permute-done.2 = f32[112,256]{1,0:T(8,128)S(1)} collective-permute-done((f32[112,256]{1,0:T(8,128)S(1)}, f32[112,256]{1,0:T(8,128)S(1)}, u32[]{:S(2)}, u32[]{:S(2)}) %collective-permute-start.2) | collective-permute-done | bytes 114720 | tf_op jit(solution)/shard_map/ppermute | solution.py:27
  15.5 0.4 collective-permute-done.1
  15.9 2.5 %collective-permute-start.6 = (f32[112,256]{1,0:T(8,128)S(1)}, f32[112,256]{1,0:T(8,128)S(1)}, u32[]{:S(2)}, u32[]{:S(2)}) collective-permute-start(f32[112,256]{1,0:T(8,128)S(1)} %fusion.1), channel_id=1, source_target_pairs={{0,2},{1,3},{2,4},{3,5},{4,6},{5,7},{6,0},{7,1},{8,10},{9,11},{10,... | collective-permute-start | bytes 344072 | tf_op jit(solution)/shard_map/ppermute | solution.py:27
  18.4 2.8 %collective-permute-start.5 = (f32[112,256]{1,0:T(8,128)S(1)}, f32[112,256]{1,0:T(8,128)S(1)}, u32[]{:S(2)}, u32[]{:S(2)}) collective-permute-start(f32[112,256]{1,0:T(8,128)S(1)} %fusion.1), channel_id=1, source_target_pairs={{0,4},{1,5},{2,6},{3,7},{4,0},{5,1},{6,2},{7,3},{8,12},{9,13},{10,... | collective-permute-start | bytes 344072 | tf_op jit(solution)/shard_map/ppermute | solution.py:27
  21.2 0.3 collective-permute-start.4
  21.6 1.2 %collective-permute-done.6 = f32[112,256]{1,0:T(8,128)S(1)} collective-permute-done((f32[112,256]{1,0:T(8,128)S(1)}, f32[112,256]{1,0:T(8,128)S(1)}, u32[]{:S(2)}, u32[]{:S(2)}) %collective-permute-start.6) | collective-permute-done | bytes 114720 | tf_op jit(solution)/shard_map/ppermute | solution.py:27
  22.8 2.1 %collective-permute-done.5 = f32[112,256]{1,0:T(8,128)S(1)} collective-permute-done((f32[112,256]{1,0:T(8,128)S(1)}, f32[112,256]{1,0:T(8,128)S(1)}, u32[]{:S(2)}, u32[]{:S(2)}) %collective-permute-start.5) | collective-permute-done | bytes 114720 | tf_op jit(solution)/shard_map/ppermute | solution.py:27
  24.9 1.2 %collective-permute-done.4 = f32[112,256]{1,0:T(8,128)S(1)} collective-permute-done((f32[112,256]{1,0:T(8,128)S(1)}, f32[112,256]{1,0:T(8,128)S(1)}, u32[]{:S(2)}, u32[]{:S(2)}) %collective-permute-start.4) | collective-permute-done | bytes 114720 | tf_op jit(solution)/shard_map/ppermute | solution.py:27
  26.1 0.1 collective-permute-start.7
  26.2 1.3 %project_own.1 = (bf16[448,256]{1,0:T(8,128)(2,1)S(1)}, bf16[448,256]{1,0:T(8,128)(2,1)S(1)}, f32[1024,256]{1,0:T(8,128)S(1)}, f32[256,256]{1,0:T(8,128)S(1)}) custom-call(bf16[448,1024]{1,0:T(8,128)(2,1)S(1)} %get-tuple-element.47.s_high.s0_high, bf16[448,1024]{1,0:T(8,128)(2,1)S(1)} %get-tuple-element.48.s_low.s0_low, f32[448,256]{1,0:T(8,128)S(1)} %pad_maximum_fusion.own_ref), custom_call_target="tpu_custom_call" | custom-call | flops 880803840 | bytes 4194304 | tf_op jit(solution)/shard_map/project_own/pallas_call | solution.py:183
  27.5 0.5 collective-permute-done.7.other_ref
  28.0 1.2 %project_far.1 = (bf16[448,256]{1,0:T(8,128)(2,1)S(1)}, bf16[448,256]{1,0:T(8,128)(2,1)S(1)}, f32[256,256]{1,0:T(8,128)S(1)}, f32[160,256]{1,0:T(8,128)S(1)}, f32[160,256]{1,0:T(8,128)S(1)}) custom-call(s32[4]{0:T(128)S(1)} %pad_add_fusion.pos_ref, bf16[448,1024]{1,0:T(8,128)(2,1)S(1)} %get-tuple-element.49.s_high.s1_high, ...), custom_call_target="tpu_custom_call" | custom-call | tf_op jit(solution)/shard_map/project_far/pallas_call | solution.py:229
  29.3 3.3 %collective-permute-start.9 = (f32[160,256]{1,0:T(8,128)S(1)}, f32[160,256]{1,0:T(8,128)S(1)}, u32[]{:S(2)}, u32[]{:S(2)}) collective-permute-start(f32[160,256]{1,0:T(8,128)S(1)} %get-tuple-element.61), channel_id=1, source_target_pairs={{0,192},{8,200},{16,208},{24,216},{32,224},{40,232},{48,240},{56,2... | collective-permute-start | bytes 491528 | tf_op jit(solution)/shard_map/ppermute | solution.py:27
  32.6 1.5 %project.1 = (f32[160,256]{1,0:T(8,128)S(1)}, f32[160,256]{1,0:T(8,128)S(1)}, f32[160,256]{1,0:T(8,128)S(1)}, f32[160,256]{1,0:T(8,128)S(1)}, f32[160,256]{1,0:T(8,128)S(1)}, /*index=5*/f32[160,256]{1,0:T(8,128)S(1)}) custom-call(s32[4]{0:T(128)S(1)} %pad_add_fusion.pos_ref, bf16[448,1024]{1,0:T(8,128)(2,1)S(1)} %get-tuple-element.49.s_high.s1_high, ...), custom_call_target="tpu_custom_call" | custom-call | flops 528482304 | bytes 4194304 | tf_op jit(solution)/shard_map/project/pallas_call | solution.py:256
  34.0 0.8 collective-permute-start.8
  34.9 1.4 %collective-permute-done.9 = f32[160,256]{1,0:T(8,128)S(1)} collective-permute-done((f32[160,256]{1,0:T(8,128)S(1)}, f32[160,256]{1,0:T(8,128)S(1)}, u32[]{:S(2)}, u32[]{:S(2)}) %collective-permute-start.9) | collective-permute-done | bytes 163872 | tf_op jit(solution)/shard_map/ppermute | solution.py:27
  36.3 3.8 %collective-permute-start.10 = (f32[160,256]{1,0:T(8,128)S(1)}, f32[160,256]{1,0:T(8,128)S(1)}, u32[]{:S(2)}, u32[]{:S(2)}) collective-permute-start(f32[160,256]{1,0:T(8,128)S(1)} %add.82), channel_id=1, source_target_pairs={{0,192},{8,200},{16,208},{24,216},{32,224},{40,232},{48,240},{56,2... | collective-permute-start | bytes 491528 | tf_op jit(solution)/shard_map/ppermute | solution.py:27
  40.1 0.1 collective-permute-start.11
  40.2 0.7 collective-permute-done.12
  40.9 1.4 %collective-permute-start.13 = (f32[160,256]{1,0:T(8,128)S(1)}, f32[160,256]{1,0:T(8,128)S(1)}, u32[]{:S(2)}, u32[]{:S(2)}) collective-permute-start(f32[160,256]{1,0:T(8,128)S(1)} %add.85), channel_id=1, source_target_pairs={{0,64},{8,72},{16,80},{24,88},{32,96},{40,104},{48,112},{56,120},{... | collective-permute-start | bytes 491528 | tf_op jit(solution)/shard_map/ppermute | solution.py:27
  42.2 1.0 collective-permute-done.8
  43.3 1.5 %collective-permute-done.10 = f32[160,256]{1,0:T(8,128)S(1)} collective-permute-done((f32[160,256]{1,0:T(8,128)S(1)}, f32[160,256]{1,0:T(8,128)S(1)}, u32[]{:S(2)}, u32[]{:S(2)}) %collective-permute-start.10) | collective-permute-done | bytes 163872 | tf_op jit(solution)/shard_map/ppermute | solution.py:27
  44.8 5.9 %collective-permute-start.16 = (f32[80,256]{1,0:T(8,128)S(1)}, f32[80,256]{1,0:T(8,128)S(1)}, u32[]{:S(2)}, u32[]{:S(2)}) collective-permute-start(f32[80,256]{1,0:T(8,128)S(1)} %slice.87), channel_id=1, source_target_pairs={{0,56},{8,0},{16,8},{24,16},{32,24},{40,32},{48,40},{56,48},{64,12... | collective-permute-start | bytes 245768 | tf_op jit(solution)/shard_map/ppermute | solution.py:27
  50.7 0.0 collective-permute-done.11
  50.7 0.0 collective-permute-done.13
  50.8 0.1 collective-permute-start.15
  50.9 1.9 %collective-permute-start.14 = (f32[80,256]{1,0:T(8,128)S(1)}, f32[80,256]{1,0:T(8,128)S(1)}, u32[]{:S(2)}, u32[]{:S(2)}) collective-permute-start(f32[80,256]{1,0:T(8,128)S(1)} %get-tuple-element.87), channel_id=1, source_target_pairs={{0,16},{8,24},{16,32},{24,40},{32,48},{40,56},{48,0},{56,8},{64,80... | collective-permute-start | bytes 245768 | tf_op jit(solution)/shard_map/ppermute | solution.py:27
  52.8 0.0 collective-permute-done.16
  52.8 3.7 %collective-permute-done.15 = f32[80,256]{1,0:T(8,128)S(1)} collective-permute-done((f32[80,256]{1,0:T(8,128)S(1)}, f32[80,256]{1,0:T(8,128)S(1)}, u32[]{:S(2)}, u32[]{:S(2)}) %collective-permute-start.15) | collective-permute-done | bytes 81952 | tf_op jit(solution)/shard_map/ppermute | solution.py:27
  56.5 2.6 %collective-permute-done.14 = f32[80,256]{1,0:T(8,128)S(1)} collective-permute-done((f32[80,256]{1,0:T(8,128)S(1)}, f32[80,256]{1,0:T(8,128)S(1)}, u32[]{:S(2)}, u32[]{:S(2)}) %collective-permute-start.14) | collective-permute-done | bytes 81952 | tf_op jit(solution)/shard_map/ppermute | solution.py:27
  59.1 4.4 %collective-permute-start.17 = (f32[80,256]{1,0:T(8,128)S(1)}, f32[80,256]{1,0:T(8,128)S(1)}, u32[]{:S(2)}, u32[]{:S(2)}) collective-permute-start(f32[80,256]{1,0:T(8,128)S(1)} %fusion.2), channel_id=1, source_target_pairs={{0,32},{8,40},{16,48},{24,56},{32,0},{40,8},{48,16},{56,24},{64,96... | collective-permute-start | bytes 245768 | tf_op jit(solution)/shard_map/ppermute | solution.py:27
  63.5 4.9 %collective-permute-done.17 = f32[80,256]{1,0:T(8,128)S(1)} collective-permute-done((f32[80,256]{1,0:T(8,128)S(1)}, f32[80,256]{1,0:T(8,128)S(1)}, u32[]{:S(2)}, u32[]{:S(2)}) %collective-permute-start.17) | collective-permute-done | bytes 81952 | tf_op jit(solution)/shard_map/ppermute | solution.py:27
  68.5 0.1 collective-permute-start.20
  68.5 0.5 collective-permute-start.19
  69.1 1.5 %collective-permute-start.18 = (f32[80,256]{1,0:T(8,128)S(1)}, f32[80,256]{1,0:T(8,128)S(1)}, u32[]{:S(2)}, u32[]{:S(2)}) collective-permute-start(f32[80,256]{1,0:T(8,128)S(1)} %add.90), channel_id=1, source_target_pairs={{0,8},{8,16},{16,24},{24,32},{32,40},{40,48},{48,56},{56,0},{64,72... | collective-permute-start | bytes 245768 | tf_op jit(solution)/shard_map/ppermute | solution.py:27
  70.6 2.4 %collective-permute-done.20 = f32[80,256]{1,0:T(8,128)S(1)} collective-permute-done((f32[80,256]{1,0:T(8,128)S(1)}, f32[80,256]{1,0:T(8,128)S(1)}, u32[]{:S(2)}, u32[]{:S(2)}) %collective-permute-start.20) | collective-permute-done | bytes 81952 | tf_op jit(solution)/shard_map/ppermute | solution.py:27
  73.0 3.1 %collective-permute-done.19 = f32[80,256]{1,0:T(8,128)S(1)} collective-permute-done((f32[80,256]{1,0:T(8,128)S(1)}, f32[80,256]{1,0:T(8,128)S(1)}, u32[]{:S(2)}, u32[]{:S(2)}) %collective-permute-start.19) | collective-permute-done | bytes 81952 | tf_op jit(solution)/shard_map/ppermute | solution.py:27
  76.1 0.9 collective-permute-done.18
  77.0 4.1 %collective-permute-start.26 = (f32[64,256]{1,0:T(8,128)S(1)}, f32[64,256]{1,0:T(8,128)S(1)}, u32[]{:S(2)}, u32[]{:S(2)}) collective-permute-start(f32[64,256]{1,0:T(8,128)S(1)} %pad_maximum_fusion.2.p0), channel_id=1, source_target_pairs={{0,192},{8,200},{16,208},{24,216},{32,224},{40,232},{48,240},{56,2... | collective-permute-start | bytes 196616 | tf_op jit(solution)/shard_map/ppermute | solution.py:27
  81.0 0.0 collective-permute-start.25
  81.0 1.0 collective-permute-start.24
  82.0 2.4 %collective-permute-start.23 = (f32[256,256]{1,0:T(8,128)S(1)}, f32[256,256]{1,0:T(8,128)S(1)}, u32[]{:S(2)}, u32[]{:S(2)}) collective-permute-start(f32[256,256]{1,0:T(8,128)S(1)} %pad_maximum_fusion.1.p0), channel_id=1, source_target_pairs={{0,192},{8,200},{16,208},{24,216},{32,224},{40,232},{48,240},{56,2... | collective-permute-start | bytes 786440 | tf_op jit(solution)/shard_map/ppermute | solution.py:27
  84.4 2.3 %collective-permute-start.22 = (f32[256,256]{1,0:T(8,128)S(1)}, f32[256,256]{1,0:T(8,128)S(1)}, u32[]{:S(2)}, u32[]{:S(2)}) collective-permute-start(f32[256,256]{1,0:T(8,128)S(1)} %pad_maximum_fusion.1.p0), channel_id=1, source_target_pairs={{0,128},{8,136},{16,144},{24,152},{32,160},{40,168},{48,176},{56,1... | collective-permute-start | bytes 786440 | tf_op jit(solution)/shard_map/ppermute | solution.py:27
  86.7 0.0 collective-permute-done.26.p3
  86.7 0.0 collective-permute-start.21
  86.7 0.8 collective-permute-done.25.p2
  87.6 0.4 collective-permute-done.24.p1
  88.0 9.3 %factor.1.inverse_ref = f32[256,256]{1,0:T(8,128)S(1)} custom-call(s32[4]{0:T(128)S(1)} %pad_add_fusion.pos_ref, f32[64,256]{1,0:T(8,128)S(1)} %pad_maximum_fusion.2.p0, f32[64,256]{1,0:T(8,128)S(1)} %collective-permute-done.24.p1, f32[64,256]{1,0:T(8,128)S(1)} %collective-permute-done.25.p2, f32[64,256]{1,0:T(8,128)S(1)} %collective-permute-done.26.p3), custom_call_target="tpu_custom_call" | custom-call | flops 10737418240 | bytes 33554432 | tf_op jit(solution)/shard_map/factor/pallas_call | solution.py:366
  97.3 1.3 %coefficients.1 = (f32[1024,256]{1,0:T(8,128)S(1)}, f32[1,256]{1,0:T(1,128)S(1)}) custom-call(s32[4]{0:T(128)S(1)} %pad_add_fusion.pos_ref, f32[256,256]{1,0:T(8,128)S(1)} %pad_maximum_fusion.1.p0, f32[256,256]{1,0:T(8,128)S(1)} %collective-permute-done.21.p1, f32[256,256]{1,0:T(8,128)S(1)} %collective-permute-done.22.p2, ...), custom_call_target="tpu_custom_call" | custom-call | tf_op jit(solution)/shard_map/coefficients/pallas_call | solution.py:412
  98.6 0.1 collective-permute-start.27
  98.7 0.8 orthonormal.1
  99.6 0.3 collective-permute-done.27
  99.9 1.5 %collective-permute-start.30 = (f32[1,256]{1,0:T(1,128)S(1)}, f32[1,256]{1,0:T(1,128)S(1)}, u32[]{:S(2)}, u32[]{:S(2)}) collective-permute-start(f32[1,256]{1,0:T(1,128)S(1)} %add.91), channel_id=1, source_target_pairs={{0,6},{1,7},{2,0},{3,1},{4,2},{5,3},{6,4},{7,5},{8,14},{9,15},{10,... | collective-permute-start | bytes 3080 | tf_op jit(solution)/shard_map/ppermute | solution.py:27
  101.4 1.2 %collective-permute-start.29 = (f32[1,256]{1,0:T(1,128)S(1)}, f32[1,256]{1,0:T(1,128)S(1)}, u32[]{:S(2)}, u32[]{:S(2)}) collective-permute-start(f32[1,256]{1,0:T(1,128)S(1)} %add.91), channel_id=1, source_target_pairs={{0,4},{1,5},{2,6},{3,7},{4,0},{5,1},{6,2},{7,3},{8,12},{9,13},{10,... | collective-permute-start | bytes 3080 | tf_op jit(solution)/shard_map/ppermute | solution.py:27
  102.6 2.6 %collective-permute-start.28 = (f32[1,256]{1,0:T(1,128)S(1)}, f32[1,256]{1,0:T(1,128)S(1)}, u32[]{:S(2)}, u32[]{:S(2)}) collective-permute-start(f32[1,256]{1,0:T(1,128)S(1)} %add.91), channel_id=1, source_target_pairs={{0,2},{1,3},{2,4},{3,5},{4,6},{5,7},{6,0},{7,1},{8,10},{9,11},{10,... | collective-permute-start | bytes 3080 | tf_op jit(solution)/shard_map/ppermute | solution.py:27
  105.2 2.9 %feedback.1 = f32[896,1024]{1,0:T(8,128)} custom-call(s32[4]{0:T(128)S(1)} %pad_add_fusion.pos_ref, bf16[448,1024]{1,0:T(8,128)(2,1)S(1)} %get-tuple-element.47.s_high.s0_high, bf16[448,1024]{1,0:T(8,128)(2,1)S(1)} %get-tuple-element.48.s_low.s0_low, bf16[448,1024]{1,0:T(8,128)(2,1)S(1)} %get-tuple-element.49.s_high.s1_high, ...), custom_call_target="tpu_custom_call" | custom-call | flops 939524096 | bytes 10485760 | tf_op jit(solution)/shard_map/feedback/pallas_call | solution.py:449
  108.2 3.5 %update.1 = (f32[1024,256]{1,0:T(8,128)}, bf16[896,1024]{1,0:T(8,128)(2,1)}) custom-call(s32[4]{0:T(128)S(1)} %pad_add_fusion.pos_ref, bf16[896,256]{1,0:T(8,128)(2,1)S(1)} %get-tuple-element.72.q_ref.high_ref, bf16[896,256]{1,0:T(8,128)(2,1)S(1)} %get-tuple-element.76.low_ref, f32[1024,256]{1,0:T(8,128)S(1)} %get-tuple-element.69.c_ref, ...), custom_call_target="tpu_custom_call" | custom-call | tf_op jit(solution)/shard_map/update/pallas_call | solution.py:481
  (32 shorter events, 0.4 us)
Async XLA Ops:
  5.1 1.9 %collective-permute-start = (f32[448,256]{1,0:T(8,128)S(1)}, f32[448,256]{1,0:T(8,128)S(1)}, u32[]{:S(2)}, u32[]{:S(2)}) collective-permute-start(f32[448,256]{1,0:T(8,128)S(1)} %get-tuple-element.52), channel_id=1, source_target_pairs={{0,1},{1,0},{2,3},{3,2},{4,5},{5,4},{6,7},{7,6},{8,9},{9,8},{10,11... | collective-permute-start | bytes 1376264 | tf_op jit(solution)/shard_map/ppermute | solution.py:27
  7.1 5.4 %collective-permute-start.3 = (f32[112,256]{1,0:T(8,128)S(1)}, f32[112,256]{1,0:T(8,128)S(1)}, u32[]{:S(2)}, u32[]{:S(2)}) collective-permute-start(f32[112,256]{1,0:T(8,128)S(1)} %get-tuple-element.83), channel_id=1, source_target_pairs={{0,6},{1,7},{2,0},{3,1},{4,2},{5,3},{6,4},{7,5},{8,14},{9,15},{10,... | collective-permute-start | bytes 344072 | tf_op jit(solution)/shard_map/ppermute | solution.py:27
  9.4 6.0 %collective-permute-start.2 = (f32[112,256]{1,0:T(8,128)S(1)}, f32[112,256]{1,0:T(8,128)S(1)}, u32[]{:S(2)}, u32[]{:S(2)}) collective-permute-start(f32[112,256]{1,0:T(8,128)S(1)} %get-tuple-element.84), channel_id=1, source_target_pairs={{0,2},{1,3},{2,4},{3,5},{4,6},{5,7},{6,0},{7,1},{8,10},{9,11},{10,... | collective-permute-start | bytes 344072 | tf_op jit(solution)/shard_map/ppermute | solution.py:27
  9.4 6.4 %collective-permute-start.1 = (f32[112,256]{1,0:T(8,128)S(1)}, f32[112,256]{1,0:T(8,128)S(1)}, u32[]{:S(2)}, u32[]{:S(2)}) collective-permute-start(f32[112,256]{1,0:T(8,128)S(1)} %get-tuple-element.85), channel_id=1, source_target_pairs={{0,4},{1,5},{2,6},{3,7},{4,0},{5,1},{6,2},{7,3},{8,12},{9,13},{10,... | collective-permute-start | bytes 344072 | tf_op jit(solution)/shard_map/ppermute | solution.py:27
  15.9 6.9 %collective-permute-start.6 = (f32[112,256]{1,0:T(8,128)S(1)}, f32[112,256]{1,0:T(8,128)S(1)}, u32[]{:S(2)}, u32[]{:S(2)}) collective-permute-start(f32[112,256]{1,0:T(8,128)S(1)} %fusion.1), channel_id=1, source_target_pairs={{0,2},{1,3},{2,4},{3,5},{4,6},{5,7},{6,0},{7,1},{8,10},{9,11},{10,... | collective-permute-start | bytes 344072 | tf_op jit(solution)/shard_map/ppermute | solution.py:27
  18.4 6.5 %collective-permute-start.5 = (f32[112,256]{1,0:T(8,128)S(1)}, f32[112,256]{1,0:T(8,128)S(1)}, u32[]{:S(2)}, u32[]{:S(2)}) collective-permute-start(f32[112,256]{1,0:T(8,128)S(1)} %fusion.1), channel_id=1, source_target_pairs={{0,4},{1,5},{2,6},{3,7},{4,0},{5,1},{6,2},{7,3},{8,12},{9,13},{10,... | collective-permute-start | bytes 344072 | tf_op jit(solution)/shard_map/ppermute | solution.py:27
  21.2 4.9 %collective-permute-start.4 = (f32[112,256]{1,0:T(8,128)S(1)}, f32[112,256]{1,0:T(8,128)S(1)}, u32[]{:S(2)}, u32[]{:S(2)}) collective-permute-start(f32[112,256]{1,0:T(8,128)S(1)} %fusion.1), channel_id=1, source_target_pairs={{0,6},{1,7},{2,0},{3,1},{4,2},{5,3},{6,4},{7,5},{8,14},{9,15},{10,... | collective-permute-start | bytes 344072 | tf_op jit(solution)/shard_map/ppermute | solution.py:27
  26.1 1.9 %collective-permute-start.7 = (f32[448,256]{1,0:T(8,128)S(1)}, f32[448,256]{1,0:T(8,128)S(1)}, u32[]{:S(2)}, u32[]{:S(2)}) collective-permute-start(f32[448,256]{1,0:T(8,128)S(1)} %pad_maximum_fusion.own_ref), channel_id=1, source_target_pairs={{0,1},{1,0},{2,3},{3,2},{4,5},{5,4},{6,7},{7,6},{8,9},{9,8},{10,11... | collective-permute-start | bytes 1376264 | tf_op jit(solution)/shard_map/ppermute | solution.py:27
  29.3 7.0 %collective-permute-start.9 = (f32[160,256]{1,0:T(8,128)S(1)}, f32[160,256]{1,0:T(8,128)S(1)}, u32[]{:S(2)}, u32[]{:S(2)}) collective-permute-start(f32[160,256]{1,0:T(8,128)S(1)} %get-tuple-element.61), channel_id=1, source_target_pairs={{0,192},{8,200},{16,208},{24,216},{32,224},{40,232},{48,240},{56,2... | collective-permute-start | bytes 491528 | tf_op jit(solution)/shard_map/ppermute | solution.py:27
  32.6 8.3 %collective-permute-start.12 = (f32[160,256]{1,0:T(8,128)S(1)}, f32[160,256]{1,0:T(8,128)S(1)}, u32[]{:S(2)}, u32[]{:S(2)}) collective-permute-start(f32[160,256]{1,0:T(8,128)S(1)} %get-tuple-element.65), channel_id=1, source_target_pairs={{0,64},{8,72},{16,80},{24,88},{32,96},{40,104},{48,112},{56,120},{... | collective-permute-start | bytes 491528 | tf_op jit(solution)/shard_map/ppermute | solution.py:27
  34.0 9.2 %collective-permute-start.8 = (f32[160,256]{1,0:T(8,128)S(1)}, f32[160,256]{1,0:T(8,128)S(1)}, u32[]{:S(2)}, u32[]{:S(2)}) collective-permute-start(f32[160,256]{1,0:T(8,128)S(1)} %get-tuple-element.59), channel_id=1, source_target_pairs={{0,64},{8,72},{16,80},{24,88},{32,96},{40,104},{48,112},{56,120},{... | collective-permute-start | bytes 491528 | tf_op jit(solution)/shard_map/ppermute | solution.py:27
  36.3 8.4 %collective-permute-start.10 = (f32[160,256]{1,0:T(8,128)S(1)}, f32[160,256]{1,0:T(8,128)S(1)}, u32[]{:S(2)}, u32[]{:S(2)}) collective-permute-start(f32[160,256]{1,0:T(8,128)S(1)} %add.82), channel_id=1, source_target_pairs={{0,192},{8,200},{16,208},{24,216},{32,224},{40,232},{48,240},{56,2... | collective-permute-start | bytes 491528 | tf_op jit(solution)/shard_map/ppermute | solution.py:27
  40.1 10.6 %collective-permute-start.11 = (f32[160,256]{1,0:T(8,128)S(1)}, f32[160,256]{1,0:T(8,128)S(1)}, u32[]{:S(2)}, u32[]{:S(2)}) collective-permute-start(f32[160,256]{1,0:T(8,128)S(1)} %get-tuple-element.63), channel_id=1, source_target_pairs={{0,192},{8,200},{16,208},{24,216},{32,224},{40,232},{48,240},{56,2... | collective-permute-start | bytes 491528 | tf_op jit(solution)/shard_map/ppermute | solution.py:27
  40.9 9.9 %collective-permute-start.13 = (f32[160,256]{1,0:T(8,128)S(1)}, f32[160,256]{1,0:T(8,128)S(1)}, u32[]{:S(2)}, u32[]{:S(2)}) collective-permute-start(f32[160,256]{1,0:T(8,128)S(1)} %add.85), channel_id=1, source_target_pairs={{0,64},{8,72},{16,80},{24,88},{32,96},{40,104},{48,112},{56,120},{... | collective-permute-start | bytes 491528 | tf_op jit(solution)/shard_map/ppermute | solution.py:27
  44.8 8.0 %collective-permute-start.16 = (f32[80,256]{1,0:T(8,128)S(1)}, f32[80,256]{1,0:T(8,128)S(1)}, u32[]{:S(2)}, u32[]{:S(2)}) collective-permute-start(f32[80,256]{1,0:T(8,128)S(1)} %slice.87), channel_id=1, source_target_pairs={{0,56},{8,0},{16,8},{24,16},{32,24},{40,32},{48,40},{56,48},{64,12... | collective-permute-start | bytes 245768 | tf_op jit(solution)/shard_map/ppermute | solution.py:27
  50.8 5.7 %collective-permute-start.15 = (f32[80,256]{1,0:T(8,128)S(1)}, f32[80,256]{1,0:T(8,128)S(1)}, u32[]{:S(2)}, u32[]{:S(2)}) collective-permute-start(f32[80,256]{1,0:T(8,128)S(1)} %get-tuple-element.86), channel_id=1, source_target_pairs={{0,8},{8,16},{16,24},{24,32},{32,40},{40,48},{48,56},{56,0},{64,72... | collective-permute-start | bytes 245768 | tf_op jit(solution)/shard_map/ppermute | solution.py:27
  50.9 8.2 %collective-permute-start.14 = (f32[80,256]{1,0:T(8,128)S(1)}, f32[80,256]{1,0:T(8,128)S(1)}, u32[]{:S(2)}, u32[]{:S(2)}) collective-permute-start(f32[80,256]{1,0:T(8,128)S(1)} %get-tuple-element.87), channel_id=1, source_target_pairs={{0,16},{8,24},{16,32},{24,40},{32,48},{40,56},{48,0},{56,8},{64,80... | collective-permute-start | bytes 245768 | tf_op jit(solution)/shard_map/ppermute | solution.py:27
  59.1 9.3 %collective-permute-start.17 = (f32[80,256]{1,0:T(8,128)S(1)}, f32[80,256]{1,0:T(8,128)S(1)}, u32[]{:S(2)}, u32[]{:S(2)}) collective-permute-start(f32[80,256]{1,0:T(8,128)S(1)} %fusion.2), channel_id=1, source_target_pairs={{0,32},{8,40},{16,48},{24,56},{32,0},{40,8},{48,16},{56,24},{64,96... | collective-permute-start | bytes 245768 | tf_op jit(solution)/shard_map/ppermute | solution.py:27
  68.5 4.5 %collective-permute-start.20 = (f32[80,256]{1,0:T(8,128)S(1)}, f32[80,256]{1,0:T(8,128)S(1)}, u32[]{:S(2)}, u32[]{:S(2)}) collective-permute-start(f32[80,256]{1,0:T(8,128)S(1)} %add.90), channel_id=1, source_target_pairs={{0,56},{8,0},{16,8},{24,16},{32,24},{40,32},{48,40},{56,48},{64,12... | collective-permute-start | bytes 245768 | tf_op jit(solution)/shard_map/ppermute | solution.py:27
  68.5 7.5 %collective-permute-start.19 = (f32[80,256]{1,0:T(8,128)S(1)}, f32[80,256]{1,0:T(8,128)S(1)}, u32[]{:S(2)}, u32[]{:S(2)}) collective-permute-start(f32[80,256]{1,0:T(8,128)S(1)} %add.90), channel_id=1, source_target_pairs={{0,16},{8,24},{16,32},{24,40},{32,48},{40,56},{48,0},{56,8},{64,80... | collective-permute-start | bytes 245768 | tf_op jit(solution)/shard_map/ppermute | solution.py:27
  69.1 7.9 %collective-permute-start.18 = (f32[80,256]{1,0:T(8,128)S(1)}, f32[80,256]{1,0:T(8,128)S(1)}, u32[]{:S(2)}, u32[]{:S(2)}) collective-permute-start(f32[80,256]{1,0:T(8,128)S(1)} %add.90), channel_id=1, source_target_pairs={{0,8},{8,16},{16,24},{24,32},{32,40},{40,48},{48,56},{56,0},{64,72... | collective-permute-start | bytes 245768 | tf_op jit(solution)/shard_map/ppermute | solution.py:27
  77.0 9.8 %collective-permute-start.26 = (f32[64,256]{1,0:T(8,128)S(1)}, f32[64,256]{1,0:T(8,128)S(1)}, u32[]{:S(2)}, u32[]{:S(2)}) collective-permute-start(f32[64,256]{1,0:T(8,128)S(1)} %pad_maximum_fusion.2.p0), channel_id=1, source_target_pairs={{0,192},{8,200},{16,208},{24,216},{32,224},{40,232},{48,240},{56,2... | collective-permute-start | bytes 196616 | tf_op jit(solution)/shard_map/ppermute | solution.py:27
  81.0 6.5 %collective-permute-start.25 = (f32[64,256]{1,0:T(8,128)S(1)}, f32[64,256]{1,0:T(8,128)S(1)}, u32[]{:S(2)}, u32[]{:S(2)}) collective-permute-start(f32[64,256]{1,0:T(8,128)S(1)} %pad_maximum_fusion.2.p0), channel_id=1, source_target_pairs={{0,128},{8,136},{16,144},{24,152},{32,160},{40,168},{48,176},{56,1... | collective-permute-start | bytes 196616 | tf_op jit(solution)/shard_map/ppermute | solution.py:27
  81.0 6.9 %collective-permute-start.24 = (f32[64,256]{1,0:T(8,128)S(1)}, f32[64,256]{1,0:T(8,128)S(1)}, u32[]{:S(2)}, u32[]{:S(2)}) collective-permute-start(f32[64,256]{1,0:T(8,128)S(1)} %pad_maximum_fusion.2.p0), channel_id=1, source_target_pairs={{0,64},{8,72},{16,80},{24,88},{32,96},{40,104},{48,112},{56,120},{... | collective-permute-start | bytes 196616 | tf_op jit(solution)/shard_map/ppermute | solution.py:27
  82.0 15.2 %collective-permute-start.23 = (f32[256,256]{1,0:T(8,128)S(1)}, f32[256,256]{1,0:T(8,128)S(1)}, u32[]{:S(2)}, u32[]{:S(2)}) collective-permute-start(f32[256,256]{1,0:T(8,128)S(1)} %pad_maximum_fusion.1.p0), channel_id=1, source_target_pairs={{0,192},{8,200},{16,208},{24,216},{32,224},{40,232},{48,240},{56,2... | collective-permute-start | bytes 786440 | tf_op jit(solution)/shard_map/ppermute | solution.py:27
  84.4 12.9 %collective-permute-start.22 = (f32[256,256]{1,0:T(8,128)S(1)}, f32[256,256]{1,0:T(8,128)S(1)}, u32[]{:S(2)}, u32[]{:S(2)}) collective-permute-start(f32[256,256]{1,0:T(8,128)S(1)} %pad_maximum_fusion.1.p0), channel_id=1, source_target_pairs={{0,128},{8,136},{16,144},{24,152},{32,160},{40,168},{48,176},{56,1... | collective-permute-start | bytes 786440 | tf_op jit(solution)/shard_map/ppermute | solution.py:27
  86.7 10.6 %collective-permute-start.21 = (f32[256,256]{1,0:T(8,128)S(1)}, f32[256,256]{1,0:T(8,128)S(1)}, u32[]{:S(2)}, u32[]{:S(2)}) collective-permute-start(f32[256,256]{1,0:T(8,128)S(1)} %pad_maximum_fusion.1.p0), channel_id=1, source_target_pairs={{0,64},{8,72},{16,80},{24,88},{32,96},{40,104},{48,112},{56,120},{... | collective-permute-start | bytes 786440 | tf_op jit(solution)/shard_map/ppermute | solution.py:27
  98.6 1.2 %collective-permute-start.27 = (f32[1,256]{1,0:T(1,128)S(1)}, f32[1,256]{1,0:T(1,128)S(1)}, u32[]{:S(2)}, u32[]{:S(2)}) collective-permute-start(f32[1,256]{1,0:T(1,128)S(1)} %get-tuple-element.66), channel_id=1, source_target_pairs={{0,1},{1,0},{2,3},{3,2},{4,5},{5,4},{6,7},{7,6},{8,9},{9,8},{10,11... | collective-permute-start | bytes 3080 | tf_op jit(solution)/shard_map/ppermute | solution.py:27
  99.9 8.3 %collective-permute-start.30 = (f32[1,256]{1,0:T(1,128)S(1)}, f32[1,256]{1,0:T(1,128)S(1)}, u32[]{:S(2)}, u32[]{:S(2)}) collective-permute-start(f32[1,256]{1,0:T(1,128)S(1)} %add.91), channel_id=1, source_target_pairs={{0,6},{1,7},{2,0},{3,1},{4,2},{5,3},{6,4},{7,5},{8,14},{9,15},{10,... | collective-permute-start | bytes 3080 | tf_op jit(solution)/shard_map/ppermute | solution.py:27
  101.4 6.8 %collective-permute-start.29 = (f32[1,256]{1,0:T(1,128)S(1)}, f32[1,256]{1,0:T(1,128)S(1)}, u32[]{:S(2)}, u32[]{:S(2)}) collective-permute-start(f32[1,256]{1,0:T(1,128)S(1)} %add.91), channel_id=1, source_target_pairs={{0,4},{1,5},{2,6},{3,7},{4,0},{5,1},{6,2},{7,3},{8,12},{9,13},{10,... | collective-permute-start | bytes 3080 | tf_op jit(solution)/shard_map/ppermute | solution.py:27
  102.6 5.6 %collective-permute-start.28 = (f32[1,256]{1,0:T(1,128)S(1)}, f32[1,256]{1,0:T(1,128)S(1)}, u32[]{:S(2)}, u32[]{:S(2)}) collective-permute-start(f32[1,256]{1,0:T(1,128)S(1)} %add.91), channel_id=1, source_target_pairs={{0,2},{1,3},{2,4},{3,5},{4,6},{5,7},{6,0},{7,1},{8,10},{9,11},{10,... | collective-permute-start | bytes 3080 | tf_op jit(solution)/shard_map/ppermute | solution.py:27
